TPU v7x, 32 devices: a whole 2x2x4 slice. The times are simulated.
32 devices in a mesh: star: 4 (over y, x), tm: 8 (over z, core).
Axes of the slice: x: 2, y: 2, z: 4, core: 2. Of those that a mesh axis runs over, the one named last changes fastest.
Arguments:
- astro_coef: float32 [4, 5, 8192], P('star', None, 'tm'), may hold values from -1.5 to 1.5
- star_index: int32 [4, 8192], P('star', 'tm'), may hold values from 0 to 2047
- att_coef: float32 [4, 64, 64, 128], P('star', 'tm'), may hold values from -0.26516503 to 0.26516503
- att_start: int32 [4, 64], P('star', 'tm'), may hold values from 0 to 255, as said below
- inst_coef: float32 [4, 6, 8192], P('star', None, 'tm'), may hold values from -0.61237246 to 0.61237246
- inst_index: int32 [4, 6, 8192], P('star', None, 'tm'), may hold values from 0 to 1023
- observed: float32 [4, 8192], P('star', 'tm'), may hold values from -6 to 6
Outputs:
- solution_astro: float32 [5, 8192], P(None, ('star', 'tm'))
- solution_att: float32 [2048], P('tm')
- solution_inst: float32 [1024], replicated
Inputs may be any that keep to these rules, and one draw needn't show every extreme that they name: `att_start`: within each time range, block b starts between 32 * b and 32 * b + 31, so starts increase with the block; the last block of every range starts at 255, so its unknowns run into the next time range.
All inputs are finite; a program needn't handle non-finite values.
Results may differ from a plain program's by a relative error of at most 0.00021.
Values sent between devices are 32-bit elements; how exact they have to be, the bound alone decides.
No kernel may reach another device: no remote copies, remote signals or barrier semaphores. Data moves between devices by JAX's collectives and lax.ppermute only.
A program may use at most 64 MiB of HBM per device.

v0:
```python
import functools

import jax
import jax.numpy as jnp
from jax import lax
from jax.experimental import pallas as pl
from jax.experimental.pallas import tpu as pltpu
from jax.sharding import PartitionSpec as P

STARS_DEV = 2048
NINST = 1024
ITERS = 3
ATT_DEV = 256
LANES = 128

epsilon = 1e-06
f32 = jnp.float32
bf16 = jnp.bfloat16
VMEM_LIMIT = 16 * 1024 * 1024


def halves(value):
    top = value.astype(bf16).astype(f32)
    return top, (value - top).astype(bf16).astype(f32)


def dot_lanes(left, right):
    return lax.dot_general(left, right, (((1,), (1,)), ((), ())), preferred_element_type=f32)


def dot_plain(left, right):
    return lax.dot_general(left, right, (((1,), (0,)), ((), ())), preferred_element_type=f32)


def lane_pick(row, lane_index):
    table = jnp.broadcast_to(row, lane_index.shape)
    return jnp.take_along_axis(table, lane_index, axis=1, mode="promise_in_bounds")


def table_pick(rows, index):
    high, low = index >> 7, index & (LANES - 1)
    total = jnp.zeros(index.shape, f32)
    for place, row in enumerate(rows):
        total = jnp.where(high == place, lane_pick(row, low), total)
    return total


def one_hot_low(index_row):
    shape = (LANES, LANES)
    low = jnp.broadcast_to(index_row & (LANES - 1), shape)
    hit = lax.broadcasted_iota(jnp.int32, shape, 0) == low
    return jnp.where(hit, 1.0, 0.0).astype(bf16)


def spread_high(index_row, value_row, count):
    shape = (count, LANES)
    high = jnp.broadcast_to(index_row >> 7, shape)
    hit = lax.broadcasted_iota(jnp.int32, shape, 0) == high
    return jnp.where(hit, jnp.broadcast_to(value_row, shape), 0.0)


def block_masks(blocks, width):
    shape = (blocks, LANES)
    row = lax.broadcasted_iota(jnp.int32, shape, 0)
    lane = lax.broadcasted_iota(jnp.int32, shape, 1)
    per_tile = LANES // width
    tiles = blocks // per_tile
    return [row == tile * per_tile + lane // width for tile in range(tiles)], row, lane


def inst_back(rows, coef_ref, index_ref, table_ref, spread_ref):
    slots, blocks = len(coef_ref), rows.shape[0]
    count = NINST // LANES
    for slot in range(slots):
        top, rest = halves(coef_ref[slot][...] * rows)
        index = index_ref[slot][...]
        for block in range(blocks):
            here = slice(block, block + 1)
            pieces = [spread_high(index[here], part[here], count) for part in (top, rest)]
            at = (slot * blocks + block) * LANES
            spread_ref[:, at : at + LANES] = jnp.concatenate(pieces, axis=0).astype(bf16)
    both = dot_lanes(spread_ref[...], table_ref[...])
    return both[:count] + both[count:]


def att_back(rows, att2, starts, width):
    blocks = rows.shape[0]
    size = att2.shape[0] // 2
    top, rest = halves(rows)
    both = dot_lanes(jnp.concatenate([top, rest], axis=0).astype(bf16), att2)
    both = both[:blocks] + both[blocks:]
    both = both[:, :size] + both[:, size:]
    masks, row, lane = block_masks(blocks, width)
    own = jnp.zeros((blocks, LANES), f32)
    for tile, mask in enumerate(masks):
        own = own + jnp.where(mask, both[:, tile * LANES : (tile + 1) * LANES], 0.0)
    shift = (row % (LANES // width)) * width
    out = []
    for tile in range((ATT_DEV + width + LANES - 1) // LANES):
        offset = lane + tile * LANES - starts
        inside = (offset >= 0) & (offset < width)
        picked = jnp.take_along_axis(
            own, jnp.where(inside, offset + shift, 0), axis=1, mode="promise_in_bounds"
        )
        out.append(jnp.sum(jnp.where(inside, picked, 0.0), axis=0, keepdims=True))
    return jnp.concatenate(out, axis=0)


def att_forward(att_rows, att2, starts, width):
    blocks = starts.shape[0]
    masks, row, lane = block_masks(blocks, width)
    tiles = [att_rows[tile : tile + 1] for tile in range(att_rows.shape[0])]
    window = table_pick(tiles, starts + lane % width)
    wide = jnp.concatenate([jnp.where(mask, window, 0.0) for mask in masks], axis=1)
    top, rest = halves(wide)
    left = jnp.concatenate([top, rest], axis=0).astype(bf16)
    both = dot_plain(jnp.concatenate([left, left], axis=1), att2)
    return both[:blocks] + both[blocks:]


def first_kernel(width, b_hbm, astro_hbm, star_hbm, att_hbm, starts_hbm, coef_hbm, index_hbm,
                 send_ref, table_ref, att2_ref, floats_ref, ints_ref,
                 b_ref, astro_ref, star_ref, att_ref, starts_ref, coef_ref, index_ref,
                 spread_ref, sems):
    pairs = [(index_hbm, index_ref), (coef_hbm, coef_ref), (b_hbm, b_ref), (starts_hbm, starts_ref),
             (att_hbm, att_ref), (astro_hbm, astro_ref), (star_hbm, star_ref)]
    copies = [
        pltpu.make_async_copy(source, target, sems.at[place])
        for place, (source, target) in enumerate(pairs)
    ]
    for copy in copies:
        copy.start()
    copies[0].wait()
    slots, blocks, _ = index_ref.shape
    comps = astro_ref.shape[0]
    for slot in range(slots):
        index = index_ref[slot]
        ints_ref[16 + slot * 8 : 24 + slot * 8] = index
        for block in range(blocks):
            at = (slot * blocks + block) * LANES
            table_ref[:, at : at + LANES] = one_hot_low(index[block : block + 1])
    for copy in copies[1:]:
        copy.wait()
    rows = b_ref[...]
    att = att_ref[...]
    top = att.astype(bf16)
    att2_ref[...] = jnp.concatenate([top, (att - top.astype(f32)).astype(bf16)], axis=0)
    shape = (blocks, LANES)
    starts_row = jnp.broadcast_to(starts_ref[...].astype(f32), (blocks, blocks))
    diagonal = lax.broadcasted_iota(jnp.int32, (blocks, blocks), 0) == lax.broadcasted_iota(
        jnp.int32, (blocks, blocks), 1
    )
    starts = jnp.sum(jnp.where(diagonal, starts_row, 0.0), axis=1, keepdims=True)
    starts = jnp.broadcast_to(starts.astype(jnp.int32), shape)
    ints_ref[0:8] = star_ref[...]
    ints_ref[8:16] = starts
    send_ref[0:8] = rows
    coefs = [coef_ref.at[slot] for slot in range(slots)]
    indices = [index_ref.at[slot] for slot in range(slots)]
    send_ref[8:16] = inst_back(rows, coefs, indices, table_ref, spread_ref)
    send_ref[16:19] = att_back(rows, att2_ref[...], starts, width)
    send_ref[19:20] = jnp.sum(rows * rows, axis=0, keepdims=True)
    send_ref[20:24] = jnp.zeros((4, LANES), f32)
    for comp in range(comps):
        send_ref[24 + comp * 8 : 32 + comp * 8] = astro_ref[comp]
        floats_ref[comp * 8 : comp * 8 + 8] = astro_ref[comp]
    send_ref[24 + comps * 8 : 32 + comps * 8] = star_ref[...].astype(f32)
    for slot in range(slots):
        at = (comps + slot) * 8
        floats_ref[at : at + 8] = coef_ref[slot]


def tree_sum(values):
    while len(values) > 1:
        values = [values[i] + values[i + 1] for i in range(0, len(values), 2)]
    return values[0]


def chip_kernel(count, *refs):
    ins, out_ref = refs[:count], refs[count]
    chip = lax.axis_index("tm") // 2
    extra = ins[0].shape[0] - 24
    base = 8 * count + 16
    for gap in range(count):
        where = chip ^ gap
        out_ref[pl.ds(pl.multiple_of(where * 8, 8), 8)] = ins[gap][0:8]
        out_ref[pl.ds(pl.multiple_of(base + where * 8, 8), 8)] = ins[gap][16:24]
        if extra:
            at = pl.multiple_of(base + 8 * count + where * extra, 8)
            out_ref[pl.ds(at, extra)] = ins[gap][24:]
    out_ref[8 * count : 8 * count + 8] = tree_sum([ref[8:16] for ref in ins])
    out_ref[8 * count + 8 : base] = tree_sum([ref[16:24] for ref in ins])


def group_kernel(count, own_ref, other_ref, out_ref):
    me = lax.axis_index("tm")
    chip, core = me // 2, me % 2
    low = 8 * count
    base = low + 16

    def part(ref, where):
        where = jnp.clip(where, 0, count - 1)
        return ref[pl.ds(pl.multiple_of(base + where * 8, 8), 8)]

    mine = part(own_ref, chip)
    prev = part(other_ref, chip - 1 + core)
    after = part(other_ref, chip + core)
    half = lax.broadcasted_iota(jnp.int32, (1, LANES), 1) < 64
    first = mine[0:1] + jnp.where(half & (me > 0), prev[2:3], 0.0)
    last = jnp.where(half & (me < 2 * count - 1), mine[2:3] + after[0:1], 0.0)
    scalars = own_ref[low + 8 : low + 16] + other_ref[low + 8 : low + 16]
    out_ref[0:8] = own_ref[low : low + 8] + other_ref[low : low + 8]
    out_ref[8:16] = jnp.concatenate([first, mine[1:2], last, scalars[3:8]], axis=0)


def astro_kernel(first, count, *refs):
    high = STARS_DEV // LANES
    if first:
        keep, (out_ref, table_ref, spread_ref) = refs[:2], refs[2:]
        ins = keep
    else:
        keep, table_ref, ins, (out_ref, spread_ref) = refs[:2], refs[2], refs[3:5], refs[5:]
    base = 16 * count + 16
    extra = (keep[0].shape[0] - base) // count
    comps = extra // 8 - 1
    long = 8 * LANES

    def one(place, total):
        for half in range(2):
            rows = ins[half][pl.ds(pl.multiple_of(place * 8, 8), 8)]
            packed = keep[half][pl.ds(pl.multiple_of(base + place * extra, 8), extra)]
            index = packed[comps * 8 :].astype(jnp.int32)
            at0 = pl.multiple_of((half * count + place) * long, long)
            split = [halves(packed[comp * 8 : comp * 8 + 8] * rows) for comp in range(comps)]
            for block in range(8):
                here = slice(block, block + 1)
                if first:
                    table_ref[:, pl.ds(at0 + block * LANES, LANES)] = one_hot_low(index[here])
                pieces = []
                for part in range(2):
                    for comp in range(comps):
                        pieces.append(spread_high(index[here], split[comp][part][here], high))
                spread_ref[half, :, block * LANES : (block + 1) * LANES] = jnp.concatenate(
                    pieces, axis=0
                ).astype(bf16)
            total = total + dot_lanes(spread_ref[half], table_ref[:, pl.ds(at0, long)])
        return total

    total = lax.fori_loop(0, count, one, jnp.zeros((2 * comps * high, LANES), f32))
    out_ref[...] = total[: comps * high] + total[comps * high :]


def sum_kernel(*refs):
    refs[-1][...] = tree_sum([ref[...] for ref in refs[:-1]])


def lane_sum(row):
    return jnp.broadcast_to(jnp.sum(row, axis=1, keepdims=True), row.shape)


def next_bidiagonal(total, state):
    squares, mixed, size = (lane_sum(total[row : row + 1]) for row in (11, 12, 13))
    alpha2 = size + epsilon
    alpha = jnp.sqrt(alpha2)
    rest = jnp.maximum(squares / alpha2 - 2.0 * mixed + alpha2 * state[0:1], 0.0)
    beta2 = rest + epsilon
    return alpha, jnp.sqrt(beta2), rest / beta2


def step_kernel(step, width, tm_count, star_count, *refs):
    floats_ref, ints_ref, att2_ref, table_ref, sum_ref, rows_ref = refs[:6]
    refs = refs[6:]
    if step > 0:
        state_ref, old_z_ref, old_g_ref, old_u_ref = refs[:4]
        refs = refs[4:]
    gathered, refs = refs[:star_count], refs[star_count:]
    send_ref, state_out, z_ref, g_ref, u_ref, s_ref, spread_ref = refs
    high = STARS_DEV // LANES
    comps = sum_ref.shape[0] // high
    blocks = 8
    slots = floats_ref.shape[0] // 8 - comps
    coef_ref = [floats_ref.at[(comps + slot) * 8 : (comps + slot) * 8 + 8] for slot in range(slots)]
    index_ref = [ints_ref.at[16 + slot * 8 : 24 + slot * 8] for slot in range(slots)]
    total = tree_sum([ref[...] for ref in gathered])
    back = jnp.concatenate([sum_ref[...], total[0:8], total[8:16]], axis=0)
    if step == 0:
        squares = lane_sum(total[11:12])
        beta2 = squares + epsilon
        beta = jnp.sqrt(beta2)
        u = rows_ref[0:8] / beta
        g = back / beta
        z = g
        state_out[...] = jnp.concatenate(
            [squares / beta2, beta, jnp.zeros((14, LANES), f32)], axis=0
        )
        left2 = squares / beta2
    else:
        state = state_ref[...]
        alpha, beta, left2 = next_bidiagonal(total, state)
        u = (rows_ref[...] / alpha - alpha * old_u_ref[...]) / beta
        g = (back / alpha - alpha * old_g_ref[...]) / beta
        z = g - (beta / alpha) * old_z_ref[...]
        pieces = [left2, state[1 : 1 + step], beta]
        pieces += [jnp.zeros((7 - step, LANES), f32)] + ([state[9 : 8 + step]] if step > 1 else [])
        pieces += [alpha, jnp.zeros((15 - 8 - step + 1 - 1, LANES), f32)]
        state_out[...] = jnp.concatenate(pieces, axis=0)
    z_ref[...] = z
    g_ref[...] = g
    u_ref[...] = u
    base = comps * high
    inst_rows = z[base : base + 8]
    att_rows = z[base + 8 : base + 11]
    starts = ints_ref[8:16]
    rows = att_forward(att_rows, att2_ref[...], starts, width)
    star = ints_ref[0:8]
    star_high, star_low = star >> 7, star & (LANES - 1)
    for comp in range(comps):
        picked = jnp.zeros((blocks, LANES), f32)
        for place in range(high):
            at = comp * high + place
            picked = jnp.where(star_high == place, lane_pick(z[at : at + 1], star_low), picked)
        rows = rows + floats_ref[comp * 8 : comp * 8 + 8] * picked
    pieces = [inst_rows[place : place + 1] for place in range(8)]
    for slot in range(slots):
        rows = rows + coef_ref[slot][...] * table_pick(pieces, index_ref[slot][...])
    s_ref[...] = rows
    astro_z = z[:base]
    size = jnp.sum(astro_z * astro_z, axis=0, keepdims=True) * (1.0 / tm_count)
    own = att_rows[: ATT_DEV // LANES]
    size = size + jnp.sum(own * own, axis=0, keepdims=True) * (1.0 / star_count)
    size = size + jnp.sum(inst_rows * inst_rows, axis=0, keepdims=True) * (
        1.0 / (star_count * tm_count)
    )
    scalars = [
        jnp.sum(rows * rows, axis=0, keepdims=True),
        jnp.sum(rows * u, axis=0, keepdims=True),
        size,
        jnp.zeros((2, LANES), f32),
    ]
    if step == ITERS - 1:
        send_ref[...] = jnp.concatenate([jnp.zeros((3, LANES), f32)] + scalars, axis=0)
        return
    send_ref[0:8] = rows
    send_ref[8:16] = inst_back(rows, coef_ref, index_ref, table_ref, spread_ref)
    att = att_back(rows, att2_ref[...], starts, width)
    send_ref[16:24] = jnp.concatenate([att] + scalars, axis=0)


def last_kernel(comps, share, star_count, state_ref, *refs):
    gathered, refs = refs[:star_count], refs[star_count:]
    z_refs = refs[:ITERS]
    astro_ref, att_ref, inst_ref = refs[ITERS:]
    high = STARS_DEV // LANES
    me = lax.axis_index("tm")
    total = tree_sum([ref[...] for ref in gathered])
    total = jnp.concatenate([jnp.zeros((11, LANES), f32), total[3:8]], axis=0)
    state = state_ref[...]
    alpha, beta, _ = next_bidiagonal(total, state)
    betas = [state[1 + k : 2 + k] for k in range(ITERS)] + [beta]
    alphas = [state[9 + k : 10 + k] for k in range(ITERS - 1)] + [alpha]
    rho_bar, phi_bar = alphas[0], betas[0]
    weights = [jnp.zeros((1, LANES), f32)] * ITERS
    search = [jnp.zeros((1, LANES), f32)] * ITERS
    search[0] = 1.0 / alphas[0]
    for k in range(ITERS):
        rho = jnp.sqrt(rho_bar * rho_bar + betas[k + 1] * betas[k + 1])
        cosine, sine = rho_bar / rho, betas[k + 1] / rho
        phi = cosine * phi_bar
        phi_bar = sine * phi_bar
        weights = [x + phi / rho * w for x, w in zip(weights, search)]
        if k + 1 < ITERS:
            theta = sine * alphas[k + 1]
            rho_bar = -cosine * alphas[k + 1]
            search = [-(theta / rho) * w for w in search]
            search[k + 1] = 1.0 / alphas[k + 1]
    base = comps * high
    tiles = share // LANES

    def mix(read):
        total = weights[0] * read(z_refs[0])
        for k in range(1, ITERS):
            total = total + weights[k] * read(z_refs[k])
        return total

    for comp in range(comps):
        for tile in range(tiles):
            at = comp * high + me * tiles + tile
            astro_ref[comp : comp + 1, tile * LANES : (tile + 1) * LANES] = mix(
                lambda ref: ref[pl.ds(at, 1)]
            )
    inst_ref[...] = mix(lambda ref: ref[base : base + 8])
    att_ref[...] = mix(lambda ref: ref[base + 8 : base + 8 + ATT_DEV // LANES])


def call(kernel, name, out, args, scratch=(), space=pltpu.VMEM):
    vmem = pl.BlockSpec(memory_space=pltpu.VMEM)
    return pl.pallas_call(
        kernel,
        name=name,
        out_shape=[jax.ShapeDtypeStruct(shape, dtype) for shape, dtype in out],
        in_specs=[pl.BlockSpec(memory_space=space)] * len(args),
        out_specs=[vmem] * len(out),
        scratch_shapes=list(scratch),
        compiler_params=pltpu.CompilerParams(vmem_limit_bytes=VMEM_LIMIT),
    )(*args)


def exchange(value, axis, gaps):
    count = lax.axis_size(axis)
    return [value] + [
        lax.ppermute(value, axis, [(i, i ^ gap) for i in range(count)]) for gap in gaps
    ]


def per_device(astro_coef, star_index, att_coef, att_start, inst_coef, inst_index, observed):
    tm_count, star_count = lax.axis_size("tm"), lax.axis_size("star")
    comps = astro_coef.shape[1]
    slots = inst_coef.shape[1]
    blocks, width, height = att_coef.shape[1:]
    share = STARS_DEV // tm_count
    high = STARS_DEV // LANES
    chips = tm_count // 2
    far = [2 * gap for gap in range(1, chips)]
    args = [
        observed.reshape(blocks, height),
        astro_coef.reshape(comps, blocks, height),
        star_index.reshape(blocks, height),
        att_coef.reshape(blocks * width, height),
        att_start,
        inst_coef.reshape(slots, blocks, height),
        inst_index.reshape(slots, blocks, height),
    ]
    long = slots * blocks * height
    extra = 8 * comps + 8
    spread = pltpu.VMEM((16, long), bf16)
    send, table, att2, floats, ints = call(
        functools.partial(first_kernel, width),
        "first",
        [((24 + extra, LANES), f32), ((LANES, long), bf16), ((2 * blocks * width, height), bf16),
         ((8 * (comps + slots), LANES), f32), ((16 + 8 * slots, LANES), jnp.int32)],
        [pltpu.with_memory_space_constraint(arg, pltpu.HBM) for arg in args],
        [pltpu.VMEM(arg.shape, arg.dtype) for arg in args]
        + [spread, pltpu.SemaphoreType.DMA((len(args),))],
        pltpu.HBM,
    )
    rows = send
    keep = star_table = state = z = g = u = None
    kept = []
    for step in range(ITERS):
        size = 16 * chips + 16 + (chips * extra if step == 0 else 0)
        (gathered,) = call(
            functools.partial(chip_kernel, chips),
            "chip",
            [((size, LANES), f32)],
            exchange(send, "tm", far),
        )
        pair = exchange(gathered, "tm", [1])
        (group,) = call(
            functools.partial(group_kernel, chips), "group", [((16, LANES), f32)], pair
        )
        across = exchange(group, "star", range(1, star_count))
        wide = [pltpu.VMEM((2, 2 * comps * high, blocks * height), bf16)]
        sums_type = ((comps * high, LANES), f32)
        if step == 0:
            keep = pair
            sums, star_table = call(
                functools.partial(astro_kernel, True, chips),
                "astro",
                [sums_type, ((LANES, tm_count * blocks * height), bf16)],
                pair,
                wide,
            )
        else:
            (sums,) = call(
                functools.partial(astro_kernel, False, chips),
                "astro",
                [sums_type],
                keep + [star_table] + pair,
                wide,
            )
        tall = comps * high + 16
        older = [] if step == 0 else [state, z, g, u]
        send, state, z, g, u, rows = call(
            functools.partial(step_kernel, step, width, tm_count, star_count),
            "step",
            [((24 if step < ITERS - 1 else 8, LANES), f32), ((16, LANES), f32),
             ((tall, LANES), f32), ((tall, LANES), f32),
             ((blocks, height), f32), ((blocks, height), f32)],
            [floats, ints, att2, table, sums, rows] + older + across,
            [spread],
        )
        kept.append(z)
    low = [((8, LANES), f32)]
    for gaps in (far, [1]):
        (send,) = call(sum_kernel, "sum", low, exchange(send, "tm", gaps))
    across = exchange(send, "star", range(1, star_count))
    out_astro, out_att, out_inst = call(
        functools.partial(last_kernel, comps, share, star_count),
        "last",
        [((comps, share), f32), ((ATT_DEV // LANES, LANES), f32), ((NINST // LANES, LANES), f32)],
        [state] + across + kept,
    )
    return out_astro, out_att.reshape(-1), out_inst.reshape(-1)


def solution(mesh):
    return jax.shard_map(
        per_device,
        mesh=mesh,
        in_specs=(
            P("star", None, "tm"),
            P("star", "tm"),
            P("star", "tm", None, None),
            P("star", "tm"),
            P("star", None, "tm"),
            P("star", None, "tm"),
            P("star", "tm"),
        ),
        out_specs=(P(None, ("star", "tm")), P("tm"), P()),
        check_vma=False,
    )
```

profile of v0, /device:TPU:0, one launch (start us, length us, event | category | flops | bytes accessed | tf_op | source)
XLA Modules:
  0.0 65.7 jit_solution(1459747969007269539)
XLA Ops:
  0.6 1.9 %first.1 = (f32[72,128]{1,0:T(8,128)S(1)}, bf16[128,6144]{1,0:T(8,128)(2,1)S(1)}, bf16[1024,128]{1,0:T(8,128)(2,1)S(1)}, f32[88,128]{1,0:T(8,128)S(1)}, s32[64,128]{1,0:T(8,128)S(1)}) custom-call(f32[8,128]{1,0:T(8,128)} %bitcast.12, f32[5,8,128]{2,1,0:T(8,128)} %bitcast.11, s32[8,128]{1,0:T(8,128)} %bitcast.13, f32[512,128]{1,0:T(8,128)} %bitcast.8, ...), custom_call_target="tpu_custom_call" | custom-call | tf_op jit(solution)/shard_map/first/pallas_call | solution.py:397
  2.6 5.1 %collective-permute-start.2 = (f32[72,128]{1,0:T(8,128)S(1)}, f32[72,128]{1,0:T(8,128)S(1)}, u32[]{:S(2)}, u32[]{:S(2)}) collective-permute-start(f32[72,128]{1,0:T(8,128)S(1)} %get-tuple-element.32.refs_0_.refs_5_), channel_id=1, source_target_pairs={{0,6},{1,7},{2,4},{3,5},{4,2},{5,3},{6,0},{7,1},{8,14},{9,15},{10,... | collective-permute-start | bytes 110600 | tf_op jit(solution)/shard_map/ppermute | solution.py:411
  7.7 0.6 collective-permute-start
  8.3 1.3 %collective-permute-done.2.refs_3_ = f32[72,128]{1,0:T(8,128)S(1)} collective-permute-done((f32[72,128]{1,0:T(8,128)S(1)}, f32[72,128]{1,0:T(8,128)S(1)}, u32[]{:S(2)}, u32[]{:S(2)}) %collective-permute-start.2) | collective-permute-done | bytes 36896 | tf_op jit(solution)/shard_map/ppermute | solution.py:411
  9.6 2.9 %collective-permute-done.1.refs_2_ = f32[72,128]{1,0:T(8,128)S(1)} collective-permute-done((f32[72,128]{1,0:T(8,128)S(1)}, f32[72,128]{1,0:T(8,128)S(1)}, u32[]{:S(2)}, u32[]{:S(2)}) %collective-permute-start.1) | collective-permute-done | bytes 36896 | tf_op jit(solution)/shard_map/ppermute | solution.py:411
  12.7 1.3 %collective-permute-done.3.refs_1_.other_ref = f32[272,128]{1,0:T(8,128)S(1)} collective-permute-done((f32[272,128]{1,0:T(8,128)S(1)}, f32[272,128]{1,0:T(8,128)S(1)}, u32[]{:S(2)}, u32[]{:S(2)}) %collective-permute-start.3) | collective-permute-done | bytes 139296 | tf_op jit(solution)/shard_map/ppermute | solution.py:411
  14.0 2.5 %collective-permute-start.6 = (f32[16,128]{1,0:T(8,128)S(1)}, f32[16,128]{1,0:T(8,128)S(1)}, u32[]{:S(2)}, u32[]{:S(2)}) collective-permute-start(f32[16,128]{1,0:T(8,128)S(1)} %group.3.refs_6_), channel_id=1, source_target_pairs={{0,24},{8,16},{16,8},{24,0},{1,25},{9,17},{17,9},{25,1},{2,26},{10... | collective-permute-start | bytes 24584 | tf_op jit(solution)/shard_map/ppermute | solution.py:411
  16.5 0.5 collective-permute-start.5
  17.0 0.5 collective-permute-start.4
  17.6 2.1 %astro.3 = (f32[80,128]{1,0:T(8,128)S(1)}, bf16[128,8192]{1,0:T(8,128)(2,1)S(1)}) custom-call(f32[272,128]{1,0:T(8,128)S(1)} %chip.3.refs_0_.own_ref, f32[272,128]{1,0:T(8,128)S(1)} %collective-permute-done.3.refs_1_.other_ref), custom_call_target="tpu_custom_call" | custom-call | tf_op jit(solution)/shard_map/astro/pallas_call | solution.py:397
  20.2 0.5 collective-permute-done.4.refs_7_
  20.7 1.1 %step.3 = (f32[24,128]{1,0:T(8,128)S(1)}, f32[16,128]{1,0:T(8,128)S(1)}, f32[96,128]{1,0:T(8,128)S(1)}, f32[96,128]{1,0:T(8,128)S(1)}, f32[8,128]{1,0:T(8,128)S(1)}, /*index=5*/f32[8,128]{1,0:T(8,128)S(1)}) custom-call(f32[88,128]{1,0:T(8,128)S(1)} %get-tuple-element.28.refs_0_, s32[64,128]{1,0:T(8,128)S(1)} %get-tuple-element.29.refs_1_, ...), custom_call_target="tpu_custom_call" | custom-call | tf_op jit(solution)/shard_map/step/pallas_call | solution.py:397
  21.8 1.5 %collective-permute-start.9 = (f32[24,128]{1,0:T(8,128)S(1)}, f32[24,128]{1,0:T(8,128)S(1)}, u32[]{:S(2)}, u32[]{:S(2)}) collective-permute-start(f32[24,128]{1,0:T(8,128)S(1)} %get-tuple-element.35.refs_0_), channel_id=1, source_target_pairs={{0,6},{1,7},{2,4},{3,5},{4,2},{5,3},{6,0},{7,1},{8,14},{9,15},{10,... | collective-permute-start | bytes 36872 | tf_op jit(solution)/shard_map/ppermute | solution.py:411
  23.3 0.6 collective-permute-start.8
  23.9 2.3 %collective-permute-start.7 = (f32[24,128]{1,0:T(8,128)S(1)}, f32[24,128]{1,0:T(8,128)S(1)}, u32[]{:S(2)}, u32[]{:S(2)}) collective-permute-start(f32[24,128]{1,0:T(8,128)S(1)} %get-tuple-element.35.refs_0_), channel_id=1, source_target_pairs={{0,2},{1,3},{2,0},{3,1},{4,6},{5,7},{6,4},{7,5},{8,10},{9,11},{10,... | collective-permute-start | bytes 36872 | tf_op jit(solution)/shard_map/ppermute | solution.py:411
  26.2 1.1 %collective-permute-done.9.refs_3_ = f32[24,128]{1,0:T(8,128)S(1)} collective-permute-done((f32[24,128]{1,0:T(8,128)S(1)}, f32[24,128]{1,0:T(8,128)S(1)}, u32[]{:S(2)}, u32[]{:S(2)}) %collective-permute-start.9) | collective-permute-done | bytes 12320 | tf_op jit(solution)/shard_map/ppermute | solution.py:411
  27.3 0.6 collective-permute-done.8.refs_2_
  28.1 1.2 %collective-permute-done.10.refs_4_.other_ref = f32[80,128]{1,0:T(8,128)S(1)} collective-permute-done((f32[80,128]{1,0:T(8,128)S(1)}, f32[80,128]{1,0:T(8,128)S(1)}, u32[]{:S(2)}, u32[]{:S(2)}) %collective-permute-start.10) | collective-permute-done | bytes 40992 | tf_op jit(solution)/shard_map/ppermute | solution.py:411
  29.3 1.6 %collective-permute-start.13 = (f32[16,128]{1,0:T(8,128)S(1)}, f32[16,128]{1,0:T(8,128)S(1)}, u32[]{:S(2)}, u32[]{:S(2)}) collective-permute-start(f32[16,128]{1,0:T(8,128)S(1)} %group.4.refs_10_), channel_id=1, source_target_pairs={{0,24},{8,16},{16,8},{24,0},{1,25},{9,17},{17,9},{25,1},{2,26},{10... | collective-permute-start | bytes 24584 | tf_op jit(solution)/shard_map/ppermute | solution.py:411
  30.8 0.5 collective-permute-start.12
  31.4 1.5 %collective-permute-start.11 = (f32[16,128]{1,0:T(8,128)S(1)}, f32[16,128]{1,0:T(8,128)S(1)}, u32[]{:S(2)}, u32[]{:S(2)}) collective-permute-start(f32[16,128]{1,0:T(8,128)S(1)} %group.4.refs_10_), channel_id=1, source_target_pairs={{0,8},{8,0},{16,24},{24,16},{1,9},{9,1},{17,25},{25,17},{2,10},{10... | collective-permute-start | bytes 24584 | tf_op jit(solution)/shard_map/ppermute | solution.py:411
  32.8 1.4 %astro.4.refs_4_ = f32[80,128]{1,0:T(8,128)S(1)} custom-call(f32[272,128]{1,0:T(8,128)S(1)} %chip.3.refs_0_.own_ref, f32[272,128]{1,0:T(8,128)S(1)} %collective-permute-done.3.refs_1_.other_ref, bf16[128,8192]{1,0:T(8,128)(2,1)S(1)} %get-tuple-element.33.refs_2_, f32[80,128]{1,0:T(8,128)S(1)} %chip.4.refs_3_.own_ref, ...), custom_call_target="tpu_custom_call" | custom-call | tf_op jit(solution)/shard_map/astro/pallas_call | solution.py:397
  34.5 0.5 collective-permute-done.11.refs_11_
  35.0 1.1 %step.4 = (f32[24,128]{1,0:T(8,128)S(1)}, f32[16,128]{1,0:T(8,128)S(1)}, f32[96,128]{1,0:T(8,128)S(1)}, f32[96,128]{1,0:T(8,128)S(1)}, f32[8,128]{1,0:T(8,128)S(1)}, /*index=5*/f32[8,128]{1,0:T(8,128)S(1)}) custom-call(f32[88,128]{1,0:T(8,128)S(1)} %get-tuple-element.28.refs_0_, s32[64,128]{1,0:T(8,128)S(1)} %get-tuple-element.29.refs_1_, ...), custom_call_target="tpu_custom_call" | custom-call | tf_op jit(solution)/shard_map/step/pallas_call | solution.py:397
  36.1 2.5 %collective-permute-start.16 = (f32[24,128]{1,0:T(8,128)S(1)}, f32[24,128]{1,0:T(8,128)S(1)}, u32[]{:S(2)}, u32[]{:S(2)}) collective-permute-start(f32[24,128]{1,0:T(8,128)S(1)} %get-tuple-element.41.refs_0_), channel_id=1, source_target_pairs={{0,6},{1,7},{2,4},{3,5},{4,2},{5,3},{6,0},{7,1},{8,14},{9,15},{10,... | collective-permute-start | bytes 36872 | tf_op jit(solution)/shard_map/ppermute | solution.py:411
  38.6 0.9 %collective-permute-start.15 = (f32[24,128]{1,0:T(8,128)S(1)}, f32[24,128]{1,0:T(8,128)S(1)}, u32[]{:S(2)}, u32[]{:S(2)}) collective-permute-start(f32[24,128]{1,0:T(8,128)S(1)} %get-tuple-element.41.refs_0_), channel_id=1, source_target_pairs={{0,4},{1,5},{2,6},{3,7},{4,0},{5,1},{6,2},{7,3},{8,12},{9,13},{10,... | collective-permute-start | bytes 36872 | tf_op jit(solution)/shard_map/ppermute | solution.py:411
  39.5 1.1 %collective-permute-start.14 = (f32[24,128]{1,0:T(8,128)S(1)}, f32[24,128]{1,0:T(8,128)S(1)}, u32[]{:S(2)}, u32[]{:S(2)}) collective-permute-start(f32[24,128]{1,0:T(8,128)S(1)} %get-tuple-element.41.refs_0_), channel_id=1, source_target_pairs={{0,2},{1,3},{2,0},{3,1},{4,6},{5,7},{6,4},{7,5},{8,10},{9,11},{10,... | collective-permute-start | bytes 36872 | tf_op jit(solution)/shard_map/ppermute | solution.py:411
  40.6 1.1 %collective-permute-done.16.refs_3_ = f32[24,128]{1,0:T(8,128)S(1)} collective-permute-done((f32[24,128]{1,0:T(8,128)S(1)}, f32[24,128]{1,0:T(8,128)S(1)}, u32[]{:S(2)}, u32[]{:S(2)}) %collective-permute-start.16) | collective-permute-done | bytes 12320 | tf_op jit(solution)/shard_map/ppermute | solution.py:411
  41.7 1.6 %collective-permute-done.15.refs_2_ = f32[24,128]{1,0:T(8,128)S(1)} collective-permute-done((f32[24,128]{1,0:T(8,128)S(1)}, f32[24,128]{1,0:T(8,128)S(1)}, u32[]{:S(2)}, u32[]{:S(2)}) %collective-permute-start.15) | collective-permute-done | bytes 12320 | tf_op jit(solution)/shard_map/ppermute | solution.py:411
  43.4 1.2 %collective-permute-done.17.refs_4_.other_ref = f32[80,128]{1,0:T(8,128)S(1)} collective-permute-done((f32[80,128]{1,0:T(8,128)S(1)}, f32[80,128]{1,0:T(8,128)S(1)}, u32[]{:S(2)}, u32[]{:S(2)}) %collective-permute-start.17) | collective-permute-done | bytes 40992 | tf_op jit(solution)/shard_map/ppermute | solution.py:411
  44.6 2.5 %collective-permute-start.20 = (f32[16,128]{1,0:T(8,128)S(1)}, f32[16,128]{1,0:T(8,128)S(1)}, u32[]{:S(2)}, u32[]{:S(2)}) collective-permute-start(f32[16,128]{1,0:T(8,128)S(1)} %group.5.refs_10_), channel_id=1, source_target_pairs={{0,24},{8,16},{16,8},{24,0},{1,25},{9,17},{17,9},{25,1},{2,26},{10... | collective-permute-start | bytes 24584 | tf_op jit(solution)/shard_map/ppermute | solution.py:411
  47.1 0.5 collective-permute-start.19
  47.6 0.5 collective-permute-start.18
  48.2 1.5 %astro.5.refs_4_ = f32[80,128]{1,0:T(8,128)S(1)} custom-call(f32[272,128]{1,0:T(8,128)S(1)} %chip.3.refs_0_.own_ref, f32[272,128]{1,0:T(8,128)S(1)} %collective-permute-done.3.refs_1_.other_ref, bf16[128,8192]{1,0:T(8,128)(2,1)S(1)} %get-tuple-element.33.refs_2_, f32[80,128]{1,0:T(8,128)S(1)} %chip.5.refs_3_.own_ref, ...), custom_call_target="tpu_custom_call" | custom-call | tf_op jit(solution)/shard_map/astro/pallas_call | solution.py:397
  49.6 1.1 %collective-permute-done.19.refs_12_ = f32[16,128]{1,0:T(8,128)S(1)} collective-permute-done((f32[16,128]{1,0:T(8,128)S(1)}, f32[16,128]{1,0:T(8,128)S(1)}, u32[]{:S(2)}, u32[]{:S(2)}) %collective-permute-start.19) | collective-permute-done | bytes 8224 | tf_op jit(solution)/shard_map/ppermute | solution.py:411
  50.8 0.5 collective-permute-done.18.refs_11_
  51.3 1.0 %step.5 = (f32[8,128]{1,0:T(8,128)S(1)}, f32[16,128]{1,0:T(8,128)S(1)}, f32[96,128]{1,0:T(8,128)S(1)}, f32[96,128]{1,0:T(8,128)}, f32[8,128]{1,0:T(8,128)}, /*index=5*/f32[8,128]{1,0:T(8,128)}) custom-call(f32[88,128]{1,0:T(8,128)S(1)} %get-tuple-element.28.refs_0_, s32[64,128]{1,0:T(8,128)S(1)} %get-tuple-element.29.refs_1_, ...), custom_call_target="tpu_custom_call" | custom-call | tf_op jit(solution)/shard_map/step/pallas_call | solution.py:397
  52.2 1.4 %collective-permute-start.23 = (f32[8,128]{1,0:T(8,128)S(1)}, f32[8,128]{1,0:T(8,128)S(1)}, u32[]{:S(2)}, u32[]{:S(2)}) collective-permute-start(f32[8,128]{1,0:T(8,128)S(1)} %get-tuple-element.48.refs_0_), channel_id=1, source_target_pairs={{0,6},{1,7},{2,4},{3,5},{4,2},{5,3},{6,0},{7,1},{8,14},{9,15},{10,... | collective-permute-start | bytes 12296 | tf_op jit(solution)/shard_map/ppermute | solution.py:411
  53.6 1.0 %collective-permute-start.22 = (f32[8,128]{1,0:T(8,128)S(1)}, f32[8,128]{1,0:T(8,128)S(1)}, u32[]{:S(2)}, u32[]{:S(2)}) collective-permute-start(f32[8,128]{1,0:T(8,128)S(1)} %get-tuple-element.48.refs_0_), channel_id=1, source_target_pairs={{0,4},{1,5},{2,6},{3,7},{4,0},{5,1},{6,2},{7,3},{8,12},{9,13},{10,... | collective-permute-start | bytes 12296 | tf_op jit(solution)/shard_map/ppermute | solution.py:411
  54.6 2.1 %collective-permute-start.21 = (f32[8,128]{1,0:T(8,128)S(1)}, f32[8,128]{1,0:T(8,128)S(1)}, u32[]{:S(2)}, u32[]{:S(2)}) collective-permute-start(f32[8,128]{1,0:T(8,128)S(1)} %get-tuple-element.48.refs_0_), channel_id=1, source_target_pairs={{0,2},{1,3},{2,0},{3,1},{4,6},{5,7},{6,4},{7,5},{8,10},{9,11},{10,... | collective-permute-start | bytes 12296 | tf_op jit(solution)/shard_map/ppermute | solution.py:411
  56.6 1.0 %collective-permute-done.23.refs_3_ = f32[8,128]{1,0:T(8,128)S(1)} collective-permute-done((f32[8,128]{1,0:T(8,128)S(1)}, f32[8,128]{1,0:T(8,128)S(1)}, u32[]{:S(2)}, u32[]{:S(2)}) %collective-permute-start.23) | collective-permute-done | bytes 4128 | tf_op jit(solution)/shard_map/ppermute | solution.py:411
  58.2 1.2 %collective-permute-done.24.refs_1_ = f32[8,128]{1,0:T(8,128)S(1)} collective-permute-done((f32[8,128]{1,0:T(8,128)S(1)}, f32[8,128]{1,0:T(8,128)S(1)}, u32[]{:S(2)}, u32[]{:S(2)}) %collective-permute-start.24) | collective-permute-done | bytes 4128 | tf_op jit(solution)/shard_map/ppermute | solution.py:411
  59.4 1.5 %collective-permute-start.27 = (f32[8,128]{1,0:T(8,128)S(1)}, f32[8,128]{1,0:T(8,128)S(1)}, u32[]{:S(2)}, u32[]{:S(2)}) collective-permute-start(f32[8,128]{1,0:T(8,128)S(1)} %sum.3.refs_0_), channel_id=1, source_target_pairs={{0,24},{8,16},{16,8},{24,0},{1,25},{9,17},{17,9},{25,1},{2,26},{10... | collective-permute-start | bytes 12296 | tf_op jit(solution)/shard_map/ppermute | solution.py:411
  60.9 0.5 collective-permute-start.26
  61.4 1.5 %collective-permute-start.25 = (f32[8,128]{1,0:T(8,128)S(1)}, f32[8,128]{1,0:T(8,128)S(1)}, u32[]{:S(2)}, u32[]{:S(2)}) collective-permute-start(f32[8,128]{1,0:T(8,128)S(1)} %sum.3.refs_0_), channel_id=1, source_target_pairs={{0,8},{8,0},{16,24},{24,16},{1,9},{9,1},{17,25},{25,17},{2,10},{10... | collective-permute-start | bytes 12296 | tf_op jit(solution)/shard_map/ppermute | solution.py:411
  62.9 1.0 %collective-permute-done.27.refs_3_ = f32[8,128]{1,0:T(8,128)S(1)} collective-permute-done((f32[8,128]{1,0:T(8,128)S(1)}, f32[8,128]{1,0:T(8,128)S(1)}, u32[]{:S(2)}, u32[]{:S(2)}) %collective-permute-start.27) | collective-permute-done | bytes 4128 | tf_op jit(solution)/shard_map/ppermute | solution.py:411
  63.9 0.6 collective-permute-done.26.refs_2_
  65.0 0.7 %last.1 = (f32[5,256]{1,0:T(8,128)}, f32[2,128]{1,0:T(2,128)}, f32[8,128]{1,0:T(8,128)}) custom-call(f32[16,128]{1,0:T(8,128)S(1)} %get-tuple-element.47.state_ref, f32[8,128]{1,0:T(8,128)S(1)} %sum.3.refs_0_, f32[8,128]{1,0:T(8,128)S(1)} %collective-permute-done.25.refs_1_, f32[8,128]{1,0:T(8,128)S(1)} %collective-permute-done.26.refs_2_, ...), custom_call_target="tpu_custom_call" | custom-call | tf_op jit(solution)/shard_map/last/pallas_call | solution.py:397
  (24 shorter events, 2.2 us)
Async XLA Ops:
  2.6 7.1 %collective-permute-start.2 = (f32[72,128]{1,0:T(8,128)S(1)}, f32[72,128]{1,0:T(8,128)S(1)}, u32[]{:S(2)}, u32[]{:S(2)}) collective-permute-start(f32[72,128]{1,0:T(8,128)S(1)} %get-tuple-element.32.refs_0_.refs_5_), channel_id=1, source_target_pairs={{0,6},{1,7},{2,4},{3,5},{4,2},{5,3},{6,0},{7,1},{8,14},{9,15},{10,... | collective-permute-start | bytes 110600 | tf_op jit(solution)/shard_map/ppermute | solution.py:411
  7.7 4.9 %collective-permute-start.1 = (f32[72,128]{1,0:T(8,128)S(1)}, f32[72,128]{1,0:T(8,128)S(1)}, u32[]{:S(2)}, u32[]{:S(2)}) collective-permute-start(f32[72,128]{1,0:T(8,128)S(1)} %get-tuple-element.32.refs_0_.refs_5_), channel_id=1, source_target_pairs={{0,4},{1,5},{2,6},{3,7},{4,0},{5,1},{6,2},{7,3},{8,12},{9,13},{10,... | collective-permute-start | bytes 110600 | tf_op jit(solution)/shard_map/ppermute | solution.py:411
  7.7 4.9 %collective-permute-start = (f32[72,128]{1,0:T(8,128)S(1)}, f32[72,128]{1,0:T(8,128)S(1)}, u32[]{:S(2)}, u32[]{:S(2)}) collective-permute-start(f32[72,128]{1,0:T(8,128)S(1)} %get-tuple-element.32.refs_0_.refs_5_), channel_id=1, source_target_pairs={{0,2},{1,3},{2,0},{3,1},{4,6},{5,7},{6,4},{7,5},{8,10},{9,11},{10,... | collective-permute-start | bytes 110600 | tf_op jit(solution)/shard_map/ppermute | solution.py:411
  12.6 1.4 %collective-permute-start.3 = (f32[272,128]{1,0:T(8,128)S(1)}, f32[272,128]{1,0:T(8,128)S(1)}, u32[]{:S(2)}, u32[]{:S(2)}) collective-permute-start(f32[272,128]{1,0:T(8,128)S(1)} %chip.3.refs_0_.own_ref), channel_id=1, source_target_pairs={{0,1},{1,0},{2,3},{3,2},{4,5},{5,4},{6,7},{7,6},{8,9},{9,8},{10,11... | collective-permute-start | bytes 417800 | tf_op jit(solution)/shard_map/ppermute | solution.py:411
  14.0 5.7 %collective-permute-start.6 = (f32[16,128]{1,0:T(8,128)S(1)}, f32[16,128]{1,0:T(8,128)S(1)}, u32[]{:S(2)}, u32[]{:S(2)}) collective-permute-start(f32[16,128]{1,0:T(8,128)S(1)} %group.3.refs_6_), channel_id=1, source_target_pairs={{0,24},{8,16},{16,8},{24,0},{1,25},{9,17},{17,9},{25,1},{2,26},{10... | collective-permute-start | bytes 24584 | tf_op jit(solution)/shard_map/ppermute | solution.py:411
  16.5 3.7 %collective-permute-start.5 = (f32[16,128]{1,0:T(8,128)S(1)}, f32[16,128]{1,0:T(8,128)S(1)}, u32[]{:S(2)}, u32[]{:S(2)}) collective-permute-start(f32[16,128]{1,0:T(8,128)S(1)} %group.3.refs_6_), channel_id=1, source_target_pairs={{0,16},{8,24},{16,0},{24,8},{1,17},{9,25},{17,1},{25,9},{2,18},{10... | collective-permute-start | bytes 24584 | tf_op jit(solution)/shard_map/ppermute | solution.py:411
  17.0 3.7 %collective-permute-start.4 = (f32[16,128]{1,0:T(8,128)S(1)}, f32[16,128]{1,0:T(8,128)S(1)}, u32[]{:S(2)}, u32[]{:S(2)}) collective-permute-start(f32[16,128]{1,0:T(8,128)S(1)} %group.3.refs_6_), channel_id=1, source_target_pairs={{0,8},{8,0},{16,24},{24,16},{1,9},{9,1},{17,25},{25,17},{2,10},{10... | collective-permute-start | bytes 24584 | tf_op jit(solution)/shard_map/ppermute | solution.py:411
  21.8 5.6 %collective-permute-start.9 = (f32[24,128]{1,0:T(8,128)S(1)}, f32[24,128]{1,0:T(8,128)S(1)}, u32[]{:S(2)}, u32[]{:S(2)}) collective-permute-start(f32[24,128]{1,0:T(8,128)S(1)} %get-tuple-element.35.refs_0_), channel_id=1, source_target_pairs={{0,6},{1,7},{2,4},{3,5},{4,2},{5,3},{6,0},{7,1},{8,14},{9,15},{10,... | collective-permute-start | bytes 36872 | tf_op jit(solution)/shard_map/ppermute | solution.py:411
  23.3 4.6 %collective-permute-start.8 = (f32[24,128]{1,0:T(8,128)S(1)}, f32[24,128]{1,0:T(8,128)S(1)}, u32[]{:S(2)}, u32[]{:S(2)}) collective-permute-start(f32[24,128]{1,0:T(8,128)S(1)} %get-tuple-element.35.refs_0_), channel_id=1, source_target_pairs={{0,4},{1,5},{2,6},{3,7},{4,0},{5,1},{6,2},{7,3},{8,12},{9,13},{10,... | collective-permute-start | bytes 36872 | tf_op jit(solution)/shard_map/ppermute | solution.py:411
  23.9 4.1 %collective-permute-start.7 = (f32[24,128]{1,0:T(8,128)S(1)}, f32[24,128]{1,0:T(8,128)S(1)}, u32[]{:S(2)}, u32[]{:S(2)}) collective-permute-start(f32[24,128]{1,0:T(8,128)S(1)} %get-tuple-element.35.refs_0_), channel_id=1, source_target_pairs={{0,2},{1,3},{2,0},{3,1},{4,6},{5,7},{6,4},{7,5},{8,10},{9,11},{10,... | collective-permute-start | bytes 36872 | tf_op jit(solution)/shard_map/ppermute | solution.py:411
  28.0 1.3 %collective-permute-start.10 = (f32[80,128]{1,0:T(8,128)S(1)}, f32[80,128]{1,0:T(8,128)S(1)}, u32[]{:S(2)}, u32[]{:S(2)}) collective-permute-start(f32[80,128]{1,0:T(8,128)S(1)} %chip.4.refs_3_.own_ref), channel_id=1, source_target_pairs={{0,1},{1,0},{2,3},{3,2},{4,5},{5,4},{6,7},{7,6},{8,9},{9,8},{10,11... | collective-permute-start | bytes 122888 | tf_op jit(solution)/shard_map/ppermute | solution.py:411
  29.3 5.0 %collective-permute-start.13 = (f32[16,128]{1,0:T(8,128)S(1)}, f32[16,128]{1,0:T(8,128)S(1)}, u32[]{:S(2)}, u32[]{:S(2)}) collective-permute-start(f32[16,128]{1,0:T(8,128)S(1)} %group.4.refs_10_), channel_id=1, source_target_pairs={{0,24},{8,16},{16,8},{24,0},{1,25},{9,17},{17,9},{25,1},{2,26},{10... | collective-permute-start | bytes 24584 | tf_op jit(solution)/shard_map/ppermute | solution.py:411
  30.8 3.7 %collective-permute-start.12 = (f32[16,128]{1,0:T(8,128)S(1)}, f32[16,128]{1,0:T(8,128)S(1)}, u32[]{:S(2)}, u32[]{:S(2)}) collective-permute-start(f32[16,128]{1,0:T(8,128)S(1)} %group.4.refs_10_), channel_id=1, source_target_pairs={{0,16},{8,24},{16,0},{24,8},{1,17},{9,25},{17,1},{25,9},{2,18},{10... | collective-permute-start | bytes 24584 | tf_op jit(solution)/shard_map/ppermute | solution.py:411
  31.4 3.7 %collective-permute-start.11 = (f32[16,128]{1,0:T(8,128)S(1)}, f32[16,128]{1,0:T(8,128)S(1)}, u32[]{:S(2)}, u32[]{:S(2)}) collective-permute-start(f32[16,128]{1,0:T(8,128)S(1)} %group.4.refs_10_), channel_id=1, source_target_pairs={{0,8},{8,0},{16,24},{24,16},{1,9},{9,1},{17,25},{25,17},{2,10},{10... | collective-permute-start | bytes 24584 | tf_op jit(solution)/shard_map/ppermute | solution.py:411
  36.1 5.6 %collective-permute-start.16 = (f32[24,128]{1,0:T(8,128)S(1)}, f32[24,128]{1,0:T(8,128)S(1)}, u32[]{:S(2)}, u32[]{:S(2)}) collective-permute-start(f32[24,128]{1,0:T(8,128)S(1)} %get-tuple-element.41.refs_0_), channel_id=1, source_target_pairs={{0,6},{1,7},{2,4},{3,5},{4,2},{5,3},{6,0},{7,1},{8,14},{9,15},{10,... | collective-permute-start | bytes 36872 | tf_op jit(solution)/shard_map/ppermute | solution.py:411
  38.6 4.7 %collective-permute-start.15 = (f32[24,128]{1,0:T(8,128)S(1)}, f32[24,128]{1,0:T(8,128)S(1)}, u32[]{:S(2)}, u32[]{:S(2)}) collective-permute-start(f32[24,128]{1,0:T(8,128)S(1)} %get-tuple-element.41.refs_0_), channel_id=1, source_target_pairs={{0,4},{1,5},{2,6},{3,7},{4,0},{5,1},{6,2},{7,3},{8,12},{9,13},{10,... | collective-permute-start | bytes 36872 | tf_op jit(solution)/shard_map/ppermute | solution.py:411
  39.5 3.8 %collective-permute-start.14 = (f32[24,128]{1,0:T(8,128)S(1)}, f32[24,128]{1,0:T(8,128)S(1)}, u32[]{:S(2)}, u32[]{:S(2)}) collective-permute-start(f32[24,128]{1,0:T(8,128)S(1)} %get-tuple-element.41.refs_0_), channel_id=1, source_target_pairs={{0,2},{1,3},{2,0},{3,1},{4,6},{5,7},{6,4},{7,5},{8,10},{9,11},{10,... | collective-permute-start | bytes 36872 | tf_op jit(solution)/shard_map/ppermute | solution.py:411
  43.3 1.3 %collective-permute-start.17 = (f32[80,128]{1,0:T(8,128)S(1)}, f32[80,128]{1,0:T(8,128)S(1)}, u32[]{:S(2)}, u32[]{:S(2)}) collective-permute-start(f32[80,128]{1,0:T(8,128)S(1)} %chip.5.refs_3_.own_ref), channel_id=1, source_target_pairs={{0,1},{1,0},{2,3},{3,2},{4,5},{5,4},{6,7},{7,6},{8,9},{9,8},{10,11... | collective-permute-start | bytes 122888 | tf_op jit(solution)/shard_map/ppermute | solution.py:411
  44.6 5.0 %collective-permute-start.20 = (f32[16,128]{1,0:T(8,128)S(1)}, f32[16,128]{1,0:T(8,128)S(1)}, u32[]{:S(2)}, u32[]{:S(2)}) collective-permute-start(f32[16,128]{1,0:T(8,128)S(1)} %group.5.refs_10_), channel_id=1, source_target_pairs={{0,24},{8,16},{16,8},{24,0},{1,25},{9,17},{17,9},{25,1},{2,26},{10... | collective-permute-start | bytes 24584 | tf_op jit(solution)/shard_map/ppermute | solution.py:411
  47.1 3.7 %collective-permute-start.19 = (f32[16,128]{1,0:T(8,128)S(1)}, f32[16,128]{1,0:T(8,128)S(1)}, u32[]{:S(2)}, u32[]{:S(2)}) collective-permute-start(f32[16,128]{1,0:T(8,128)S(1)} %group.5.refs_10_), channel_id=1, source_target_pairs={{0,16},{8,24},{16,0},{24,8},{1,17},{9,25},{17,1},{25,9},{2,18},{10... | collective-permute-start | bytes 24584 | tf_op jit(solution)/shard_map/ppermute | solution.py:411
  47.6 3.7 %collective-permute-start.18 = (f32[16,128]{1,0:T(8,128)S(1)}, f32[16,128]{1,0:T(8,128)S(1)}, u32[]{:S(2)}, u32[]{:S(2)}) collective-permute-start(f32[16,128]{1,0:T(8,128)S(1)} %group.5.refs_10_), channel_id=1, source_target_pairs={{0,8},{8,0},{16,24},{24,16},{1,9},{9,1},{17,25},{25,17},{2,10},{10... | collective-permute-start | bytes 24584 | tf_op jit(solution)/shard_map/ppermute | solution.py:411
  52.2 5.4 %collective-permute-start.23 = (f32[8,128]{1,0:T(8,128)S(1)}, f32[8,128]{1,0:T(8,128)S(1)}, u32[]{:S(2)}, u32[]{:S(2)}) collective-permute-start(f32[8,128]{1,0:T(8,128)S(1)} %get-tuple-element.48.refs_0_), channel_id=1, source_target_pairs={{0,6},{1,7},{2,4},{3,5},{4,2},{5,3},{6,0},{7,1},{8,14},{9,15},{10,... | collective-permute-start | bytes 12296 | tf_op jit(solution)/shard_map/ppermute | solution.py:411
  53.6 4.5 %collective-permute-start.22 = (f32[8,128]{1,0:T(8,128)S(1)}, f32[8,128]{1,0:T(8,128)S(1)}, u32[]{:S(2)}, u32[]{:S(2)}) collective-permute-start(f32[8,128]{1,0:T(8,128)S(1)} %get-tuple-element.48.refs_0_), channel_id=1, source_target_pairs={{0,4},{1,5},{2,6},{3,7},{4,0},{5,1},{6,2},{7,3},{8,12},{9,13},{10,... | collective-permute-start | bytes 12296 | tf_op jit(solution)/shard_map/ppermute | solution.py:411
  54.6 3.6 %collective-permute-start.21 = (f32[8,128]{1,0:T(8,128)S(1)}, f32[8,128]{1,0:T(8,128)S(1)}, u32[]{:S(2)}, u32[]{:S(2)}) collective-permute-start(f32[8,128]{1,0:T(8,128)S(1)} %get-tuple-element.48.refs_0_), channel_id=1, source_target_pairs={{0,2},{1,3},{2,0},{3,1},{4,6},{5,7},{6,4},{7,5},{8,10},{9,11},{10,... | collective-permute-start | bytes 12296 | tf_op jit(solution)/shard_map/ppermute | solution.py:411
  58.2 1.2 %collective-permute-start.24 = (f32[8,128]{1,0:T(8,128)S(1)}, f32[8,128]{1,0:T(8,128)S(1)}, u32[]{:S(2)}, u32[]{:S(2)}) collective-permute-start(f32[8,128]{1,0:T(8,128)S(1)} %sum.2.refs_0_), channel_id=1, source_target_pairs={{0,1},{1,0},{2,3},{3,2},{4,5},{5,4},{6,7},{7,6},{8,9},{9,8},{10,11... | collective-permute-start | bytes 12296 | tf_op jit(solution)/shard_map/ppermute | solution.py:411
  59.4 4.5 %collective-permute-start.27 = (f32[8,128]{1,0:T(8,128)S(1)}, f32[8,128]{1,0:T(8,128)S(1)}, u32[]{:S(2)}, u32[]{:S(2)}) collective-permute-start(f32[8,128]{1,0:T(8,128)S(1)} %sum.3.refs_0_), channel_id=1, source_target_pairs={{0,24},{8,16},{16,8},{24,0},{1,25},{9,17},{17,9},{25,1},{2,26},{10... | collective-permute-start | bytes 12296 | tf_op jit(solution)/shard_map/ppermute | solution.py:411
  60.9 3.6 %collective-permute-start.26 = (f32[8,128]{1,0:T(8,128)S(1)}, f32[8,128]{1,0:T(8,128)S(1)}, u32[]{:S(2)}, u32[]{:S(2)}) collective-permute-start(f32[8,128]{1,0:T(8,128)S(1)} %sum.3.refs_0_), channel_id=1, source_target_pairs={{0,16},{8,24},{16,0},{24,8},{1,17},{9,25},{17,1},{25,9},{2,18},{10... | collective-permute-start | bytes 12296 | tf_op jit(solution)/shard_map/ppermute | solution.py:411
  61.4 3.6 %collective-permute-start.25 = (f32[8,128]{1,0:T(8,128)S(1)}, f32[8,128]{1,0:T(8,128)S(1)}, u32[]{:S(2)}, u32[]{:S(2)}) collective-permute-start(f32[8,128]{1,0:T(8,128)S(1)} %sum.3.refs_0_), channel_id=1, source_target_pairs={{0,8},{8,0},{16,24},{24,16},{1,9},{9,1},{17,25},{25,17},{2,10},{10... | collective-permute-start | bytes 12296 | tf_op jit(solution)/shard_map/ppermute | solution.py:411
where the time goes:
time: 65.9 us; the launch traced here: 65.7 us
  starting transfers between devices  33.4 us (51%)
  waiting for transfers between devices  20.7 us (31%)
  Pallas kernels  10.9 us (17%)
  between operations  0.77 us (1%)
    ppermute x28, starting transfers between devices, exchange(): lax.ppermute(value, axis, [(i, i ^ gap) for i in range(count)])  33.4 us
    ppermute x28, waiting for transfers between devices, exchange(): lax.ppermute(value, axis, [(i, i ^ gap) for i in range(count)])  20.7 us
    pallas_call x16, Pallas kernels, call(): pl.pallas_call(kernel, name=name, out_shape=[jax.ShapeDtypeStruct(shape,...  10.9 us
  transfers between devices with their start and end apart: 28, of which 23 were waited for; matrix products, arithmetic and copies ran while one was open for 0% of the time, Pallas kernels for 8%

commit v1 on v0

--- a/solution.py
+++ b/solution.py
@@ -118,56 +118,76 @@
     return both[:blocks] + both[blocks:]
 
 
+def pack_places(slots, blocks, width):
+    at = slots * 8
+    return slice(0, at), slice(at, 2 * at), slice(2 * at, 2 * at + 8), slice(
+        2 * at + 8, 2 * at + 8 + blocks * width
+    )
+
+
+def prepare(pack_ref, index_rows, starts, places, table_ref, att2_ref, ints_ref):
+    count = index_rows.shape[0] // 8
+    ints_ref[0 : count * 8] = index_rows
+    ints_ref[count * 8 :] = starts
+    for place in range(count * 8):
+        table_ref[:, place * LANES : (place + 1) * LANES] = one_hot_low(
+            index_rows[place : place + 1]
+        )
+    att = pack_ref[places[3]]
+    top = att.astype(bf16)
+    att2_ref[...] = jnp.concatenate([top, (att - top.astype(f32)).astype(bf16)], axis=0)
+
+
 def first_kernel(width, b_hbm, astro_hbm, star_hbm, att_hbm, starts_hbm, coef_hbm, index_hbm,
-                 send_ref, table_ref, att2_ref, floats_ref, ints_ref,
-                 b_ref, astro_ref, star_ref, att_ref, starts_ref, coef_ref, index_ref,
+                 send_ref, pack_ref, table_ref, att2_ref, ints_ref,
+                 b_ref, astro_ref, star_ref, starts_ref, coef_ref, index_ref,
                  spread_ref, sems):
-    pairs = [(index_hbm, index_ref), (coef_hbm, coef_ref), (b_hbm, b_ref), (starts_hbm, starts_ref),
-             (att_hbm, att_ref), (astro_hbm, astro_ref), (star_hbm, star_ref)]
+    slots, blocks, _ = index_ref.shape
+    comps = astro_ref.shape[0]
+    places = pack_places(slots, blocks, width)
+    pairs = [(index_hbm, index_ref), (starts_hbm, starts_ref), (att_hbm, pack_ref.at[places[3]]),
+             (coef_hbm, coef_ref), (b_hbm, b_ref), (astro_hbm, astro_ref), (star_hbm, star_ref)]
     copies = [
         pltpu.make_async_copy(source, target, sems.at[place])
         for place, (source, target) in enumerate(pairs)
     ]
     for copy in copies:
         copy.start()
-    copies[0].wait()
-    slots, blocks, _ = index_ref.shape
-    comps = astro_ref.shape[0]
-    for slot in range(slots):
-        index = index_ref[slot]
-        ints_ref[16 + slot * 8 : 24 + slot * 8] = index
-        for block in range(blocks):
-            at = (slot * blocks + block) * LANES
-            table_ref[:, at : at + LANES] = one_hot_low(index[block : block + 1])
-    for copy in copies[1:]:
+    for copy in copies[:3]:
         copy.wait()
-    rows = b_ref[...]
-    att = att_ref[...]
-    top = att.astype(bf16)
-    att2_ref[...] = jnp.concatenate([top, (att - top.astype(f32)).astype(bf16)], axis=0)
-    shape = (blocks, LANES)
+    index = jnp.concatenate([index_ref[slot] for slot in range(slots)], axis=0)
     starts_row = jnp.broadcast_to(starts_ref[...].astype(f32), (blocks, blocks))
     diagonal = lax.broadcasted_iota(jnp.int32, (blocks, blocks), 0) == lax.broadcasted_iota(
         jnp.int32, (blocks, blocks), 1
     )
     starts = jnp.sum(jnp.where(diagonal, starts_row, 0.0), axis=1, keepdims=True)
-    starts = jnp.broadcast_to(starts.astype(jnp.int32), shape)
-    ints_ref[0:8] = star_ref[...]
-    ints_ref[8:16] = starts
-    send_ref[0:8] = rows
+    starts = jnp.broadcast_to(starts, (blocks, LANES))
+    pack_ref[places[1]] = index.astype(f32)
+    pack_ref[places[2]] = starts
+    starts = starts.astype(jnp.int32)
+    prepare(pack_ref, index, starts, places, table_ref, att2_ref, ints_ref)
+    for copy in copies[3:]:
+        copy.wait()
+    rows = b_ref[...]
     coefs = [coef_ref.at[slot] for slot in range(slots)]
     indices = [index_ref.at[slot] for slot in range(slots)]
+    for slot in range(slots):
+        pack_ref[slot * 8 : slot * 8 + 8] = coef_ref[slot]
+    send_ref[0:8] = rows
     send_ref[8:16] = inst_back(rows, coefs, indices, table_ref, spread_ref)
     send_ref[16:19] = att_back(rows, att2_ref[...], starts, width)
     send_ref[19:20] = jnp.sum(rows * rows, axis=0, keepdims=True)
     send_ref[20:24] = jnp.zeros((4, LANES), f32)
     for comp in range(comps):
         send_ref[24 + comp * 8 : 32 + comp * 8] = astro_ref[comp]
-        floats_ref[comp * 8 : comp * 8 + 8] = astro_ref[comp]
     send_ref[24 + comps * 8 : 32 + comps * 8] = star_ref[...].astype(f32)
-    for slot in range(slots):
-        at = (comps + slot) * 8
-        floats_ref[at : at + 8] = coef_ref[slot]
+
+
+def prepare_kernel(slots, blocks, width, pack_ref, table_ref, att2_ref, ints_ref):
+    places = pack_places(slots, blocks, width)
+    index = pack_ref[places[1]].astype(jnp.int32)
+    starts = pack_ref[places[2]].astype(jnp.int32)
+    prepare(pack_ref, index, starts, places, table_ref, att2_ref, ints_ref)
 
 
 def tree_sum(values):
@@ -176,7 +196,7 @@
     return values[0]
 
 
-def chip_kernel(count, *refs):
+def first_chip_kernel(count, *refs):
     ins, out_ref = refs[:count], refs[count]
     chip = lax.axis_index("tm") // 2
     extra = ins[0].shape[0] - 24
@@ -185,14 +205,26 @@
         where = chip ^ gap
         out_ref[pl.ds(pl.multiple_of(where * 8, 8), 8)] = ins[gap][0:8]
         out_ref[pl.ds(pl.multiple_of(base + where * 8, 8), 8)] = ins[gap][16:24]
-        if extra:
-            at = pl.multiple_of(base + 8 * count + where * extra, 8)
-            out_ref[pl.ds(at, extra)] = ins[gap][24:]
+        at = pl.multiple_of(base + 8 * count + where * extra, 8)
+        out_ref[pl.ds(at, extra)] = ins[gap][24:]
     out_ref[8 * count : 8 * count + 8] = tree_sum([ref[8:16] for ref in ins])
     out_ref[8 * count + 8 : base] = tree_sum([ref[16:24] for ref in ins])
 
 
-def group_kernel(count, own_ref, other_ref, out_ref):
+def group_rows(chip, count, mine, prev_row, after_row):
+    half = lax.broadcasted_iota(jnp.int32, (1, LANES), 1) < 64
+    first = mine[0:1] + jnp.where(half & (chip > 0), prev_row, 0.0)
+    last = jnp.where(half & (chip < count - 1), mine[4:5] + after_row, 0.0)
+    return [first, mine[1:4], last]
+
+
+def chip_parts(core, own, other):
+    low = jnp.where(core == 0, own, other)
+    top = jnp.where(core == 0, other, own)
+    return jnp.concatenate([low[0:2], low[2:3] + top[0:1], top[1:3]], axis=0)
+
+
+def first_group_kernel(count, own_ref, other_ref, out_ref):
     me = lax.axis_index("tm")
     chip, core = me // 2, me % 2
     low = 8 * count
@@ -202,32 +234,57 @@
         where = jnp.clip(where, 0, count - 1)
         return ref[pl.ds(pl.multiple_of(base + where * 8, 8), 8)]
 
-    mine = part(own_ref, chip)
-    prev = part(other_ref, chip - 1 + core)
-    after = part(other_ref, chip + core)
-    half = lax.broadcasted_iota(jnp.int32, (1, LANES), 1) < 64
-    first = mine[0:1] + jnp.where(half & (me > 0), prev[2:3], 0.0)
-    last = jnp.where(half & (me < 2 * count - 1), mine[2:3] + after[0:1], 0.0)
+    def of_core(which, where):
+        return jnp.where(core == which, part(own_ref, where), part(other_ref, where))
+
+    mine = chip_parts(core, part(own_ref, chip)[0:3], part(other_ref, chip)[0:3])
+    prev, after = of_core(1, chip - 1), of_core(0, chip + 1)
     scalars = own_ref[low + 8 : low + 16] + other_ref[low + 8 : low + 16]
     out_ref[0:8] = own_ref[low : low + 8] + other_ref[low : low + 8]
-    out_ref[8:16] = jnp.concatenate([first, mine[1:2], last, scalars[3:8]], axis=0)
+    out_ref[8:16] = jnp.concatenate(
+        group_rows(chip, count, mine, prev[2:3], after[0:1]) + [scalars[3:6]], axis=0
+    )
+
+
+def group_kernel(count, *refs):
+    ins, (rows_ref, out_ref) = refs[:count], refs[count:]
+    chip = lax.axis_index("tm") // 2
+    zero = jnp.zeros((8, LANES), f32)
+    prev, after = zero, zero
+    for gap in range(count):
+        where = chip ^ gap
+        for half in range(2):
+            at = pl.multiple_of((half * count + where) * 8, 8)
+            rows_ref[pl.ds(at, 8)] = ins[gap][half * 8 : half * 8 + 8]
+        low = ins[gap][24:32]
+        prev = jnp.where(where == chip - 1, low, prev)
+        after = jnp.where(where == chip + 1, low, after)
+    mine = ins[0][24:32]
+    scalars = tree_sum([ref[24:32] for ref in ins])
+    out_ref[0:8] = tree_sum([ref[16:24] for ref in ins])
+    out_ref[8:16] = jnp.concatenate(
+        group_rows(chip, count, mine, prev[4:5], after[0:1]) + [scalars[5:8]], axis=0
+    )
 
 
 def astro_kernel(first, count, *refs):
     high = STARS_DEV // LANES
     if first:
         keep, (out_ref, table_ref, spread_ref) = refs[:2], refs[2:]
-        ins = keep
     else:
-        keep, table_ref, ins, (out_ref, spread_ref) = refs[:2], refs[2], refs[3:5], refs[5:]
+        keep, (table_ref, rows_ref, out_ref, spread_ref) = refs[:2], refs[2:]
     base = 16 * count + 16
     extra = (keep[0].shape[0] - base) // count
     comps = extra // 8 - 1
     long = 8 * LANES
 
-    def one(place, total):
+    def one(place, totals):
+        new = []
         for half in range(2):
-            rows = ins[half][pl.ds(pl.multiple_of(place * 8, 8), 8)]
+            if first:
+                rows = keep[half][pl.ds(pl.multiple_of(place * 8, 8), 8)]
+            else:
+                rows = rows_ref[pl.ds(pl.multiple_of((half * count + place) * 8, 8), 8)]
             packed = keep[half][pl.ds(pl.multiple_of(base + place * extra, 8), extra)]
             index = packed[comps * 8 :].astype(jnp.int32)
             at0 = pl.multiple_of((half * count + place) * long, long)
@@ -243,10 +300,14 @@
                 spread_ref[half, :, block * LANES : (block + 1) * LANES] = jnp.concatenate(
                     pieces, axis=0
                 ).astype(bf16)
-            total = total + dot_lanes(spread_ref[half], table_ref[:, pl.ds(at0, long)])
-        return total
-
-    total = lax.fori_loop(0, count, one, jnp.zeros((2 * comps * high, LANES), f32))
+            new.append(
+                totals[half] + dot_lanes(spread_ref[half], table_ref[:, pl.ds(at0, long)])
+            )
+        return tuple(new)
+
+    zero = jnp.zeros((2 * comps * high, LANES), f32)
+    own, other = lax.fori_loop(0, count, one, (zero, zero))
+    total = own + other
     out_ref[...] = total[: comps * high] + total[comps * high :]
 
 
@@ -259,7 +320,7 @@
 
 
 def next_bidiagonal(total, state):
-    squares, mixed, size = (lane_sum(total[row : row + 1]) for row in (11, 12, 13))
+    squares, mixed, size = (lane_sum(total[row : row + 1]) for row in (13, 14, 15))
     alpha2 = size + epsilon
     alpha = jnp.sqrt(alpha2)
     rest = jnp.maximum(squares / alpha2 - 2.0 * mixed + alpha2 * state[0:1], 0.0)
@@ -267,83 +328,89 @@
     return alpha, jnp.sqrt(beta2), rest / beta2
 
 
-def step_kernel(step, width, tm_count, star_count, *refs):
-    floats_ref, ints_ref, att2_ref, table_ref, sum_ref, rows_ref = refs[:6]
-    refs = refs[6:]
+def step_kernel(step, width, slots, chips, star_count, *refs):
+    keep, packs, tables, att2s, ints, sum_ref = refs[:2], refs[2:4], refs[4:6], refs[6:8], refs[8:10], refs[10]
+    refs = refs[11:]
     if step > 0:
-        state_ref, old_z_ref, old_g_ref, old_u_ref = refs[:4]
-        refs = refs[4:]
+        state_ref, old_z_ref, old_g_ref, old_u_ref, old_s_ref = refs[:5]
+        refs = refs[5:]
     gathered, refs = refs[:star_count], refs[star_count:]
     send_ref, state_out, z_ref, g_ref, u_ref, s_ref, spread_ref = refs
+    me = lax.axis_index("tm")
+    chip, core = me // 2, me % 2
     high = STARS_DEV // LANES
     comps = sum_ref.shape[0] // high
     blocks = 8
-    slots = floats_ref.shape[0] // 8 - comps
-    coef_ref = [floats_ref.at[(comps + slot) * 8 : (comps + slot) * 8 + 8] for slot in range(slots)]
-    index_ref = [ints_ref.at[16 + slot * 8 : 24 + slot * 8] for slot in range(slots)]
     total = tree_sum([ref[...] for ref in gathered])
-    back = jnp.concatenate([sum_ref[...], total[0:8], total[8:16]], axis=0)
+    back = jnp.concatenate([sum_ref[...], total], axis=0)
     if step == 0:
-        squares = lane_sum(total[11:12])
+        squares = lane_sum(total[13:14])
         beta2 = squares + epsilon
         beta = jnp.sqrt(beta2)
-        u = rows_ref[0:8] / beta
+        at = pl.ds(pl.multiple_of(chip * 8, 8), 8)
+        u = jnp.concatenate([ref[at] for ref in keep], axis=0) / beta
         g = back / beta
         z = g
         state_out[...] = jnp.concatenate(
             [squares / beta2, beta, jnp.zeros((14, LANES), f32)], axis=0
         )
-        left2 = squares / beta2
     else:
         state = state_ref[...]
         alpha, beta, left2 = next_bidiagonal(total, state)
-        u = (rows_ref[...] / alpha - alpha * old_u_ref[...]) / beta
+        u = (old_s_ref[...] / alpha - alpha * old_u_ref[...]) / beta
         g = (back / alpha - alpha * old_g_ref[...]) / beta
         z = g - (beta / alpha) * old_z_ref[...]
-        pieces = [left2, state[1 : 1 + step], beta]
-        pieces += [jnp.zeros((7 - step, LANES), f32)] + ([state[9 : 8 + step]] if step > 1 else [])
-        pieces += [alpha, jnp.zeros((15 - 8 - step + 1 - 1, LANES), f32)]
+        pieces = [left2, state[1 : 1 + step], beta, jnp.zeros((7 - step, LANES), f32)]
+        pieces += [state[9 : 8 + step]] if step > 1 else []
+        pieces += [alpha, jnp.zeros((7 - step, LANES), f32)]
         state_out[...] = jnp.concatenate(pieces, axis=0)
     z_ref[...] = z
     g_ref[...] = g
     u_ref[...] = u
     base = comps * high
     inst_rows = z[base : base + 8]
-    att_rows = z[base + 8 : base + 11]
-    starts = ints_ref[8:16]
-    rows = att_forward(att_rows, att2_ref[...], starts, width)
-    star = ints_ref[0:8]
-    star_high, star_low = star >> 7, star & (LANES - 1)
-    for comp in range(comps):
-        picked = jnp.zeros((blocks, LANES), f32)
-        for place in range(high):
-            at = comp * high + place
-            picked = jnp.where(star_high == place, lane_pick(z[at : at + 1], star_low), picked)
-        rows = rows + floats_ref[comp * 8 : comp * 8 + 8] * picked
+    att_rows = z[base + 8 : base + 13]
+    extra = 8 * comps + 8
+    here = 16 * chips + 16 + chip * extra
     pieces = [inst_rows[place : place + 1] for place in range(8)]
-    for slot in range(slots):
-        rows = rows + coef_ref[slot][...] * table_pick(pieces, index_ref[slot][...])
-    s_ref[...] = rows
-    astro_z = z[:base]
-    size = jnp.sum(astro_z * astro_z, axis=0, keepdims=True) * (1.0 / tm_count)
-    own = att_rows[: ATT_DEV // LANES]
-    size = size + jnp.sum(own * own, axis=0, keepdims=True) * (1.0 / star_count)
-    size = size + jnp.sum(inst_rows * inst_rows, axis=0, keepdims=True) * (
-        1.0 / (star_count * tm_count)
-    )
-    scalars = [
-        jnp.sum(rows * rows, axis=0, keepdims=True),
-        jnp.sum(rows * u, axis=0, keepdims=True),
-        size,
-        jnp.zeros((2, LANES), f32),
-    ]
+    rows, insts, atts = [], [], []
+    for half in range(2):
+        starts = ints[half][slots * 8 :]
+        own = jnp.where(core == half, att_rows[0:3], att_rows[2:5])
+        part = att_forward(own, att2s[half][...], starts, width)
+        packed = keep[half][pl.ds(pl.multiple_of(here, 8), extra)]
+        star = packed[comps * 8 :].astype(jnp.int32)
+        star_high, star_low = star >> 7, star & (LANES - 1)
+        for comp in range(comps):
+            picked = jnp.zeros((blocks, LANES), f32)
+            for place in range(high):
+                at = comp * high + place
+                picked = jnp.where(star_high == place, lane_pick(z[at : at + 1], star_low), picked)
+            part = part + packed[comp * 8 : comp * 8 + 8] * picked
+        coefs = [packs[half].at[slot * 8 : slot * 8 + 8] for slot in range(slots)]
+        indices = [ints[half].at[slot * 8 : slot * 8 + 8] for slot in range(slots)]
+        for slot in range(slots):
+            part = part + coefs[slot][...] * table_pick(pieces, indices[slot][...])
+        rows.append(part)
+        if step < ITERS - 1:
+            insts.append(inst_back(part, coefs, indices, tables[half], spread_ref.at[half]))
+            atts.append(att_back(part, att2s[half][...], starts, width))
+    both = jnp.concatenate(rows, axis=0)
+    s_ref[...] = both
+
+    def squared(value):
+        return jnp.sum(value * value, axis=0, keepdims=True)
+
+    size = squared(z[:base]) * (1.0 / chips) + squared(att_rows[:4]) * (1.0 / star_count)
+    size = size + squared(inst_rows) * (1.0 / (star_count * chips))
+    mixed = [jnp.sum(rows[half] * u[half * 8 : half * 8 + 8], axis=0, keepdims=True) for half in range(2)]
+    scalars = [squared(rows[0]) + squared(rows[1]), mixed[0] + mixed[1], size]
     if step == ITERS - 1:
-        send_ref[...] = jnp.concatenate([jnp.zeros((3, LANES), f32)] + scalars, axis=0)
+        send_ref[...] = jnp.concatenate([jnp.zeros((5, LANES), f32)] + scalars, axis=0)
         return
-    send_ref[0:8] = rows
-    send_ref[8:16] = inst_back(rows, coef_ref, index_ref, table_ref, spread_ref)
-    att = att_back(rows, att2_ref[...], starts, width)
-    send_ref[16:24] = jnp.concatenate([att] + scalars, axis=0)
+    send_ref[0:16] = both
+    send_ref[16:24] = insts[0] + insts[1]
+    send_ref[24:32] = jnp.concatenate([chip_parts(core, *atts)] + scalars, axis=0)
 
 
 def last_kernel(comps, share, star_count, state_ref, *refs):
@@ -353,7 +420,7 @@
     high = STARS_DEV // LANES
     me = lax.axis_index("tm")
     total = tree_sum([ref[...] for ref in gathered])
-    total = jnp.concatenate([jnp.zeros((11, LANES), f32), total[3:8]], axis=0)
+    total = jnp.concatenate([jnp.zeros((8, LANES), f32), total], axis=0)
     state = state_ref[...]
     alpha, beta, _ = next_bidiagonal(total, state)
     betas = [state[1 + k : 2 + k] for k in range(ITERS)] + [beta]
@@ -389,7 +456,8 @@
                 lambda ref: ref[pl.ds(at, 1)]
             )
     inst_ref[...] = mix(lambda ref: ref[base : base + 8])
-    att_ref[...] = mix(lambda ref: ref[base + 8 : base + 8 + ATT_DEV // LANES])
+    rows = ATT_DEV // LANES
+    att_ref[...] = mix(lambda ref: ref[pl.ds(base + 8 + (me % 2) * rows, rows)])
 
 
 def call(kernel, name, out, args, scratch=(), space=pltpu.VMEM):
@@ -433,41 +501,55 @@
     long = slots * blocks * height
     extra = 8 * comps + 8
     spread = pltpu.VMEM((16, long), bf16)
-    send, table, att2, floats, ints = call(
+    prepared = [((LANES, long), bf16), ((2 * blocks * width, height), bf16),
+                ((8 * slots + 8, LANES), jnp.int32)]
+    here = [pltpu.with_memory_space_constraint(arg, pltpu.HBM) for arg in args]
+    send, pack, *mine = call(
         functools.partial(first_kernel, width),
         "first",
-        [((24 + extra, LANES), f32), ((LANES, long), bf16), ((2 * blocks * width, height), bf16),
-         ((8 * (comps + slots), LANES), f32), ((16 + 8 * slots, LANES), jnp.int32)],
-        [pltpu.with_memory_space_constraint(arg, pltpu.HBM) for arg in args],
-        [pltpu.VMEM(arg.shape, arg.dtype) for arg in args]
+        [((24 + extra, LANES), f32), ((16 * slots + 8 + blocks * width, LANES), f32)] + prepared,
+        here,
+        [pltpu.VMEM(arg.shape, arg.dtype) for arg in args if arg is not args[3]]
         + [spread, pltpu.SemaphoreType.DMA((len(args),))],
-        pltpu.HBM,
-    )
-    rows = send
-    keep = star_table = state = z = g = u = None
+        pl.ANY,
+    )
+    _, other_pack = exchange(pack, "tm", [1])
+    theirs = call(
+        functools.partial(prepare_kernel, slots, blocks, width), "prepare", prepared, [other_pack]
+    )
+    basics = [pack, other_pack] + [value for pair in zip(mine, theirs) for value in pair]
+    keep = star_table = state = z = g = u = rows = None
     kept = []
+    group_type = ((16, LANES), f32)
     for step in range(ITERS):
-        size = 16 * chips + 16 + (chips * extra if step == 0 else 0)
-        (gathered,) = call(
-            functools.partial(chip_kernel, chips),
-            "chip",
-            [((size, LANES), f32)],
-            exchange(send, "tm", far),
-        )
-        pair = exchange(gathered, "tm", [1])
-        (group,) = call(
-            functools.partial(group_kernel, chips), "group", [((16, LANES), f32)], pair
-        )
-        across = exchange(group, "star", range(1, star_count))
         wide = [pltpu.VMEM((2, 2 * comps * high, blocks * height), bf16)]
         sums_type = ((comps * high, LANES), f32)
+        got = exchange(send, "tm", far)
         if step == 0:
-            keep = pair
+            (gathered,) = call(
+                functools.partial(first_chip_kernel, chips),
+                "chip",
+                [((16 * chips + 16 + chips * extra, LANES), f32)],
+                got,
+            )
+            keep = exchange(gathered, "tm", [1])
+            (group,) = call(
+                functools.partial(first_group_kernel, chips), "group", [group_type], keep
+            )
+        else:
+            all_rows, group = call(
+                functools.partial(group_kernel, chips),
+                "group",
+                [((16 * chips, LANES), f32), group_type],
+                got,
+            )
+        across = exchange(group, "star", range(1, star_count))
+        if step == 0:
             sums, star_table = call(
                 functools.partial(astro_kernel, True, chips),
                 "astro",
                 [sums_type, ((LANES, tm_count * blocks * height), bf16)],
-                pair,
+                keep,
                 wide,
             )
         else:
@@ -475,24 +557,21 @@
                 functools.partial(astro_kernel, False, chips),
                 "astro",
                 [sums_type],
-                keep + [star_table] + pair,
+                keep + [star_table, all_rows],
                 wide,
             )
-        tall = comps * high + 16
-        older = [] if step == 0 else [state, z, g, u]
+        tall = ((comps * high + 16, LANES), f32)
+        pair = ((2 * blocks, height), f32)
+        older = [] if step == 0 else [state, z, g, u, rows]
         send, state, z, g, u, rows = call(
-            functools.partial(step_kernel, step, width, tm_count, star_count),
+            functools.partial(step_kernel, step, width, slots, chips, star_count),
             "step",
-            [((24 if step < ITERS - 1 else 8, LANES), f32), ((16, LANES), f32),
-             ((tall, LANES), f32), ((tall, LANES), f32),
-             ((blocks, height), f32), ((blocks, height), f32)],
-            [floats, ints, att2, table, sums, rows] + older + across,
-            [spread],
+            [((32 if step < ITERS - 1 else 8, LANES), f32), group_type, tall, tall, pair, pair],
+            keep + basics + [sums] + older + across,
+            [pltpu.VMEM((2, 16, long), bf16)],
         )
         kept.append(z)
-    low = [((8, LANES), f32)]
-    for gaps in (far, [1]):
-        (send,) = call(sum_kernel, "sum", low, exchange(send, "tm", gaps))
+    (send,) = call(sum_kernel, "sum", [((8, LANES), f32)], exchange(send, "tm", far))
     across = exchange(send, "star", range(1, star_count))
     out_astro, out_att, out_inst = call(
         functools.partial(last_kernel, comps, share, star_count),

time: 65.9 us -> 64.8 us (0.983)
  waiting for transfers between devices: 20.7 us -> 17.4 us
  Pallas kernels: 10.9 us -> 13.1 us
    ppermute x28 -> x26, waiting for transfers between devices: 20.7 us -> 17.4 us  [exchange(): lax.ppermute(value, axis, [(i, i ^ gap) for i in range(count)])]
    pallas_call x16 -> x14, Pallas kernels: 10.9 us -> 13.1 us  [call(): pl.pallas_call(kernel, name=name, out_shape=[jax.ShapeDtypeStruct(shape,...]
    ppermute x28 -> x26, starting transfers between devices: 33.4 us -> 33.4 us  [exchange(): lax.ppermute(value, axis, [(i, i ^ gap) for i in range(count)])]
  transfers between devices with their start and end apart: 28 -> 26, of which waited for: 23 -> 18; matrix products, arithmetic and copies ran while one was open for 0% -> 0% of each run, Pallas kernels for 8% -> 9%
where the time goes in v1:
time: 64.8 us; the launch traced here: 64.7 us
  starting transfers between devices  33.4 us (52%)
  waiting for transfers between devices  17.4 us (27%)
  Pallas kernels  13.1 us (20%)
  between operations  0.77 us (1%)
    ppermute x26, starting transfers between devices, exchange(): lax.ppermute(value, axis, [(i, i ^ gap) for i in range(count)])  33.4 us
    ppermute x26, waiting for transfers between devices, exchange(): lax.ppermute(value, axis, [(i, i ^ gap) for i in range(count)])  17.4 us
    pallas_call x14, Pallas kernels, call(): pl.pallas_call(kernel, name=name, out_shape=[jax.ShapeDtypeStruct(shape,...  13.1 us
  transfers between devices with their start and end apart: 26, of which 18 were waited for; matrix products, arithmetic and copies ran while one was open for 0% of the time, Pallas kernels for 9%

profile of v1, /device:TPU:0, one launch (start us, length us, event | category | flops | bytes accessed | tf_op | source)
XLA Modules:
  0.0 64.7 jit_solution(12968439352053634160)
XLA Ops:
  0.6 2.2 %first.1 = (f32[72,128]{1,0:T(8,128)S(1)}, f32[616,128]{1,0:T(8,128)S(1)}, bf16[128,6144]{1,0:T(8,128)(2,1)S(1)}, bf16[1024,128]{1,0:T(8,128)(2,1)S(1)}, s32[56,128]{1,0:T(8,128)S(1)}) custom-call(f32[8,128]{1,0:T(8,128)} %bitcast.12, f32[5,8,128]{2,1,0:T(8,128)} %bitcast.11, s32[8,128]{1,0:T(8,128)} %bitcast.13, f32[512,128]{1,0:T(8,128)} %bitcast.8, ...), custom_call_target="tpu_custom_call" | custom-call | tf_op jit(solution)/shard_map/first/pallas_call | solution.py:465
  2.8 0.5 collective-permute-start.4
  3.4 4.7 %collective-permute-start.2 = (f32[72,128]{1,0:T(8,128)S(1)}, f32[72,128]{1,0:T(8,128)S(1)}, u32[]{:S(2)}, u32[]{:S(2)}) collective-permute-start(f32[72,128]{1,0:T(8,128)S(1)} %get-tuple-element.35.refs_0_), channel_id=1, source_target_pairs={{0,6},{1,7},{2,4},{3,5},{4,2},{5,3},{6,0},{7,1},{8,14},{9,15},{10,... | collective-permute-start | bytes 110600 | tf_op jit(solution)/shard_map/ppermute | solution.py:479
  8.0 0.6 collective-permute-start
  8.7 1.5 %collective-permute-done.2.refs_3_ = f32[72,128]{1,0:T(8,128)S(1)} collective-permute-done((f32[72,128]{1,0:T(8,128)S(1)}, f32[72,128]{1,0:T(8,128)S(1)}, u32[]{:S(2)}, u32[]{:S(2)}) %collective-permute-start.2) | collective-permute-done | bytes 36896 | tf_op jit(solution)/shard_map/ppermute | solution.py:479
  10.2 2.7 %collective-permute-done.1.refs_2_ = f32[72,128]{1,0:T(8,128)S(1)} collective-permute-done((f32[72,128]{1,0:T(8,128)S(1)}, f32[72,128]{1,0:T(8,128)S(1)}, u32[]{:S(2)}, u32[]{:S(2)}) %collective-permute-start.1) | collective-permute-done | bytes 36896 | tf_op jit(solution)/shard_map/ppermute | solution.py:479
  13.0 1.3 %collective-permute-done.3.refs_1_.other_ref = f32[272,128]{1,0:T(8,128)S(1)} collective-permute-done((f32[272,128]{1,0:T(8,128)S(1)}, f32[272,128]{1,0:T(8,128)S(1)}, u32[]{:S(2)}, u32[]{:S(2)}) %collective-permute-start.3) | collective-permute-done | bytes 139296 | tf_op jit(solution)/shard_map/ppermute | solution.py:479
  14.4 2.5 %collective-permute-start.7 = (f32[16,128]{1,0:T(8,128)S(1)}, f32[16,128]{1,0:T(8,128)S(1)}, u32[]{:S(2)}, u32[]{:S(2)}) collective-permute-start(f32[16,128]{1,0:T(8,128)S(1)} %group.3.refs_11_), channel_id=1, source_target_pairs={{0,24},{8,16},{16,8},{24,0},{1,25},{9,17},{17,9},{25,1},{2,26},{10... | collective-permute-start | bytes 24584 | tf_op jit(solution)/shard_map/ppermute | solution.py:479
  16.9 0.5 collective-permute-start.6
  17.4 0.5 collective-permute-start.5
  17.9 2.2 %astro.3 = (f32[80,128]{1,0:T(8,128)S(1)}, bf16[128,8192]{1,0:T(8,128)(2,1)S(1)}) custom-call(f32[272,128]{1,0:T(8,128)S(1)} %chip.1.refs_0_.own_ref, f32[272,128]{1,0:T(8,128)S(1)} %collective-permute-done.3.refs_1_.other_ref), custom_call_target="tpu_custom_call" | custom-call | tf_op jit(solution)/shard_map/astro/pallas_call | solution.py:465
  20.2 0.5 prepare.1
  21.0 1.6 %step.3 = (f32[32,128]{1,0:T(8,128)S(1)}, f32[16,128]{1,0:T(8,128)S(1)}, f32[96,128]{1,0:T(8,128)S(1)}, f32[96,128]{1,0:T(8,128)S(1)}, f32[16,128]{1,0:T(8,128)S(1)}, /*index=5*/f32[16,128]{1,0:T(8,128)S(1)}) custom-call(f32[272,128]{1,0:T(8,128)S(1)} %chip.1.refs_0_.own_ref, f32[272,128]{1,0:T(8,128)S(1)} %collective-permute-done.3.refs_1_.other_ref, ...), custom_call_target="tpu_custom_call" | custom-call | tf_op jit(solution)/shard_map/step/pallas_call | solution.py:465
  22.7 1.9 %collective-permute-start.10 = (f32[32,128]{1,0:T(8,128)S(1)}, f32[32,128]{1,0:T(8,128)S(1)}, u32[]{:S(2)}, u32[]{:S(2)}) collective-permute-start(f32[32,128]{1,0:T(8,128)S(1)} %get-tuple-element.45.refs_0_), channel_id=1, source_target_pairs={{0,6},{1,7},{2,4},{3,5},{4,2},{5,3},{6,0},{7,1},{8,14},{9,15},{10,... | collective-permute-start | bytes 49160 | tf_op jit(solution)/shard_map/ppermute | solution.py:479
  24.8 2.3 %collective-permute-start.8 = (f32[32,128]{1,0:T(8,128)S(1)}, f32[32,128]{1,0:T(8,128)S(1)}, u32[]{:S(2)}, u32[]{:S(2)}) collective-permute-start(f32[32,128]{1,0:T(8,128)S(1)} %get-tuple-element.45.refs_0_), channel_id=1, source_target_pairs={{0,2},{1,3},{2,0},{3,1},{4,6},{5,7},{6,4},{7,5},{8,10},{9,11},{10,... | collective-permute-start | bytes 49160 | tf_op jit(solution)/shard_map/ppermute | solution.py:479
  27.1 1.1 %collective-permute-done.10.refs_3_ = f32[32,128]{1,0:T(8,128)S(1)} collective-permute-done((f32[32,128]{1,0:T(8,128)S(1)}, f32[32,128]{1,0:T(8,128)S(1)}, u32[]{:S(2)}, u32[]{:S(2)}) %collective-permute-start.10) | collective-permute-done | bytes 16416 | tf_op jit(solution)/shard_map/ppermute | solution.py:479
  28.3 0.9 %collective-permute-done.9.refs_2_ = f32[32,128]{1,0:T(8,128)S(1)} collective-permute-done((f32[32,128]{1,0:T(8,128)S(1)}, f32[32,128]{1,0:T(8,128)S(1)}, u32[]{:S(2)}, u32[]{:S(2)}) %collective-permute-start.9) | collective-permute-done | bytes 16416 | tf_op jit(solution)/shard_map/ppermute | solution.py:479
  29.2 2.2 %collective-permute-start.13 = (f32[16,128]{1,0:T(8,128)S(1)}, f32[16,128]{1,0:T(8,128)S(1)}, u32[]{:S(2)}, u32[]{:S(2)}) collective-permute-start(f32[16,128]{1,0:T(8,128)S(1)} %get-tuple-element.52.refs_16_), channel_id=1, source_target_pairs={{0,24},{8,16},{16,8},{24,0},{1,25},{9,17},{17,9},{25,1},{2,26},{10... | collective-permute-start | bytes 24584 | tf_op jit(solution)/shard_map/ppermute | solution.py:479
  31.4 0.5 collective-permute-start.12
  31.9 0.9 %collective-permute-start.11 = (f32[16,128]{1,0:T(8,128)S(1)}, f32[16,128]{1,0:T(8,128)S(1)}, u32[]{:S(2)}, u32[]{:S(2)}) collective-permute-start(f32[16,128]{1,0:T(8,128)S(1)} %get-tuple-element.52.refs_16_), channel_id=1, source_target_pairs={{0,8},{8,0},{16,24},{24,16},{1,9},{9,1},{17,25},{25,17},{2,10},{10... | collective-permute-start | bytes 24584 | tf_op jit(solution)/shard_map/ppermute | solution.py:479
  32.8 1.5 %astro.4.refs_10_ = f32[80,128]{1,0:T(8,128)S(1)} custom-call(f32[272,128]{1,0:T(8,128)S(1)} %chip.1.refs_0_.own_ref, f32[272,128]{1,0:T(8,128)S(1)} %collective-permute-done.3.refs_1_.other_ref, bf16[128,8192]{1,0:T(8,128)(2,1)S(1)} %get-tuple-element.43.refs_2_, f32[64,128]{1,0:T(8,128)S(1)} %get-tuple-element.46.refs_3_), custom_call_target="tpu_custom_call" | custom-call | tf_op jit(solution)/shard_map/astro/pallas_call | solution.py:465
  34.3 0.7 %collective-permute-done.12.refs_18_ = f32[16,128]{1,0:T(8,128)S(1)} collective-permute-done((f32[16,128]{1,0:T(8,128)S(1)}, f32[16,128]{1,0:T(8,128)S(1)}, u32[]{:S(2)}, u32[]{:S(2)}) %collective-permute-start.12) | collective-permute-done | bytes 8224 | tf_op jit(solution)/shard_map/ppermute | solution.py:479
  35.0 0.5 collective-permute-done.11.refs_17_
  35.5 1.6 %step.4 = (f32[32,128]{1,0:T(8,128)S(1)}, f32[16,128]{1,0:T(8,128)S(1)}, f32[96,128]{1,0:T(8,128)S(1)}, f32[96,128]{1,0:T(8,128)S(1)}, f32[16,128]{1,0:T(8,128)S(1)}, /*index=5*/f32[16,128]{1,0:T(8,128)S(1)}) custom-call(f32[272,128]{1,0:T(8,128)S(1)} %chip.1.refs_0_.own_ref, f32[272,128]{1,0:T(8,128)S(1)} %collective-permute-done.3.refs_1_.other_ref, ...), custom_call_target="tpu_custom_call" | custom-call | tf_op jit(solution)/shard_map/step/pallas_call | solution.py:465
  37.2 2.3 %collective-permute-start.16 = (f32[32,128]{1,0:T(8,128)S(1)}, f32[32,128]{1,0:T(8,128)S(1)}, u32[]{:S(2)}, u32[]{:S(2)}) collective-permute-start(f32[32,128]{1,0:T(8,128)S(1)} %get-tuple-element.53.refs_0_), channel_id=1, source_target_pairs={{0,6},{1,7},{2,4},{3,5},{4,2},{5,3},{6,0},{7,1},{8,14},{9,15},{10,... | collective-permute-start | bytes 49160 | tf_op jit(solution)/shard_map/ppermute | solution.py:479
  39.5 0.9 %collective-permute-start.15 = (f32[32,128]{1,0:T(8,128)S(1)}, f32[32,128]{1,0:T(8,128)S(1)}, u32[]{:S(2)}, u32[]{:S(2)}) collective-permute-start(f32[32,128]{1,0:T(8,128)S(1)} %get-tuple-element.53.refs_0_), channel_id=1, source_target_pairs={{0,4},{1,5},{2,6},{3,7},{4,0},{5,1},{6,2},{7,3},{8,12},{9,13},{10,... | collective-permute-start | bytes 49160 | tf_op jit(solution)/shard_map/ppermute | solution.py:479
  40.4 1.2 %collective-permute-start.14 = (f32[32,128]{1,0:T(8,128)S(1)}, f32[32,128]{1,0:T(8,128)S(1)}, u32[]{:S(2)}, u32[]{:S(2)}) collective-permute-start(f32[32,128]{1,0:T(8,128)S(1)} %get-tuple-element.53.refs_0_), channel_id=1, source_target_pairs={{0,2},{1,3},{2,0},{3,1},{4,6},{5,7},{6,4},{7,5},{8,10},{9,11},{10,... | collective-permute-start | bytes 49160 | tf_op jit(solution)/shard_map/ppermute | solution.py:479
  41.6 1.1 %collective-permute-done.16.refs_3_ = f32[32,128]{1,0:T(8,128)S(1)} collective-permute-done((f32[32,128]{1,0:T(8,128)S(1)}, f32[32,128]{1,0:T(8,128)S(1)}, u32[]{:S(2)}, u32[]{:S(2)}) %collective-permute-start.16) | collective-permute-done | bytes 16416 | tf_op jit(solution)/shard_map/ppermute | solution.py:479
  42.8 1.4 %collective-permute-done.15.refs_2_ = f32[32,128]{1,0:T(8,128)S(1)} collective-permute-done((f32[32,128]{1,0:T(8,128)S(1)}, f32[32,128]{1,0:T(8,128)S(1)}, u32[]{:S(2)}, u32[]{:S(2)}) %collective-permute-start.15) | collective-permute-done | bytes 16416 | tf_op jit(solution)/shard_map/ppermute | solution.py:479
  44.3 1.9 %collective-permute-start.19 = (f32[16,128]{1,0:T(8,128)S(1)}, f32[16,128]{1,0:T(8,128)S(1)}, u32[]{:S(2)}, u32[]{:S(2)}) collective-permute-start(f32[16,128]{1,0:T(8,128)S(1)} %get-tuple-element.60.refs_16_), channel_id=1, source_target_pairs={{0,24},{8,16},{16,8},{24,0},{1,25},{9,17},{17,9},{25,1},{2,26},{10... | collective-permute-start | bytes 24584 | tf_op jit(solution)/shard_map/ppermute | solution.py:479
  46.2 0.5 collective-permute-start.18
  46.7 1.1 %collective-permute-start.17 = (f32[16,128]{1,0:T(8,128)S(1)}, f32[16,128]{1,0:T(8,128)S(1)}, u32[]{:S(2)}, u32[]{:S(2)}) collective-permute-start(f32[16,128]{1,0:T(8,128)S(1)} %get-tuple-element.60.refs_16_), channel_id=1, source_target_pairs={{0,8},{8,0},{16,24},{24,16},{1,9},{9,1},{17,25},{25,17},{2,10},{10... | collective-permute-start | bytes 24584 | tf_op jit(solution)/shard_map/ppermute | solution.py:479
  47.9 1.5 %astro.5.refs_10_ = f32[80,128]{1,0:T(8,128)S(1)} custom-call(f32[272,128]{1,0:T(8,128)S(1)} %chip.1.refs_0_.own_ref, f32[272,128]{1,0:T(8,128)S(1)} %collective-permute-done.3.refs_1_.other_ref, bf16[128,8192]{1,0:T(8,128)(2,1)S(1)} %get-tuple-element.43.refs_2_, f32[64,128]{1,0:T(8,128)S(1)} %get-tuple-element.54.refs_3_), custom_call_target="tpu_custom_call" | custom-call | tf_op jit(solution)/shard_map/astro/pallas_call | solution.py:465
  49.4 0.5 collective-permute-done.18.refs_18_
  49.9 0.5 collective-permute-done.17.refs_17_
  50.4 1.1 %step.5 = (f32[8,128]{1,0:T(8,128)S(1)}, f32[16,128]{1,0:T(8,128)S(1)}, f32[96,128]{1,0:T(8,128)S(1)}, f32[96,128]{1,0:T(8,128)}, f32[16,128]{1,0:T(8,128)}, /*index=5*/f32[16,128]{1,0:T(8,128)}) custom-call(f32[272,128]{1,0:T(8,128)S(1)} %chip.1.refs_0_.own_ref, f32[272,128]{1,0:T(8,128)S(1)} %collective-permute-done.3.refs_1_.other_ref, ...), custom_call_target="tpu_custom_call" | custom-call | tf_op jit(solution)/shard_map/step/pallas_call | solution.py:465
  51.5 1.6 %collective-permute-start.22 = (f32[8,128]{1,0:T(8,128)S(1)}, f32[8,128]{1,0:T(8,128)S(1)}, u32[]{:S(2)}, u32[]{:S(2)}) collective-permute-start(f32[8,128]{1,0:T(8,128)S(1)} %get-tuple-element.62.refs_0_), channel_id=1, source_target_pairs={{0,6},{1,7},{2,4},{3,5},{4,2},{5,3},{6,0},{7,1},{8,14},{9,15},{10,... | collective-permute-start | bytes 12296 | tf_op jit(solution)/shard_map/ppermute | solution.py:479
  53.1 0.9 %collective-permute-start.21 = (f32[8,128]{1,0:T(8,128)S(1)}, f32[8,128]{1,0:T(8,128)S(1)}, u32[]{:S(2)}, u32[]{:S(2)}) collective-permute-start(f32[8,128]{1,0:T(8,128)S(1)} %get-tuple-element.62.refs_0_), channel_id=1, source_target_pairs={{0,4},{1,5},{2,6},{3,7},{4,0},{5,1},{6,2},{7,3},{8,12},{9,13},{10,... | collective-permute-start | bytes 12296 | tf_op jit(solution)/shard_map/ppermute | solution.py:479
  54.0 1.9 %collective-permute-start.20 = (f32[8,128]{1,0:T(8,128)S(1)}, f32[8,128]{1,0:T(8,128)S(1)}, u32[]{:S(2)}, u32[]{:S(2)}) collective-permute-start(f32[8,128]{1,0:T(8,128)S(1)} %get-tuple-element.62.refs_0_), channel_id=1, source_target_pairs={{0,2},{1,3},{2,0},{3,1},{4,6},{5,7},{6,4},{7,5},{8,10},{9,11},{10,... | collective-permute-start | bytes 12296 | tf_op jit(solution)/shard_map/ppermute | solution.py:479
  55.9 1.0 %collective-permute-done.22.refs_3_ = f32[8,128]{1,0:T(8,128)S(1)} collective-permute-done((f32[8,128]{1,0:T(8,128)S(1)}, f32[8,128]{1,0:T(8,128)S(1)}, u32[]{:S(2)}, u32[]{:S(2)}) %collective-permute-start.22) | collective-permute-done | bytes 4128 | tf_op jit(solution)/shard_map/ppermute | solution.py:479
  56.9 0.7 %collective-permute-done.21.refs_2_ = f32[8,128]{1,0:T(8,128)S(1)} collective-permute-done((f32[8,128]{1,0:T(8,128)S(1)}, f32[8,128]{1,0:T(8,128)S(1)}, u32[]{:S(2)}, u32[]{:S(2)}) %collective-permute-start.21) | collective-permute-done | bytes 4128 | tf_op jit(solution)/shard_map/ppermute | solution.py:479
  57.7 2.1 %collective-permute-start.25 = (f32[8,128]{1,0:T(8,128)S(1)}, f32[8,128]{1,0:T(8,128)S(1)}, u32[]{:S(2)}, u32[]{:S(2)}) collective-permute-start(f32[8,128]{1,0:T(8,128)S(1)} %sum.1.refs_0_), channel_id=1, source_target_pairs={{0,24},{8,16},{16,8},{24,0},{1,25},{9,17},{17,9},{25,1},{2,26},{10... | collective-permute-start | bytes 12296 | tf_op jit(solution)/shard_map/ppermute | solution.py:479
  59.8 0.5 collective-permute-start.24
  60.3 0.9 %collective-permute-start.23 = (f32[8,128]{1,0:T(8,128)S(1)}, f32[8,128]{1,0:T(8,128)S(1)}, u32[]{:S(2)}, u32[]{:S(2)}) collective-permute-start(f32[8,128]{1,0:T(8,128)S(1)} %sum.1.refs_0_), channel_id=1, source_target_pairs={{0,8},{8,0},{16,24},{24,16},{1,9},{9,1},{17,25},{25,17},{2,10},{10... | collective-permute-start | bytes 12296 | tf_op jit(solution)/shard_map/ppermute | solution.py:479
  61.2 1.0 %collective-permute-done.25.refs_3_ = f32[8,128]{1,0:T(8,128)S(1)} collective-permute-done((f32[8,128]{1,0:T(8,128)S(1)}, f32[8,128]{1,0:T(8,128)S(1)}, u32[]{:S(2)}, u32[]{:S(2)}) %collective-permute-start.25) | collective-permute-done | bytes 4128 | tf_op jit(solution)/shard_map/ppermute | solution.py:479
  62.2 1.2 %collective-permute-done.24.refs_2_ = f32[8,128]{1,0:T(8,128)S(1)} collective-permute-done((f32[8,128]{1,0:T(8,128)S(1)}, f32[8,128]{1,0:T(8,128)S(1)}, u32[]{:S(2)}, u32[]{:S(2)}) %collective-permute-start.24) | collective-permute-done | bytes 4128 | tf_op jit(solution)/shard_map/ppermute | solution.py:479
  63.4 0.5 collective-permute-done.23.refs_1_
  63.9 0.7 %last.1 = (f32[5,256]{1,0:T(8,128)}, f32[2,128]{1,0:T(2,128)}, f32[8,128]{1,0:T(8,128)}) custom-call(f32[16,128]{1,0:T(8,128)S(1)} %get-tuple-element.61.state_ref, f32[8,128]{1,0:T(8,128)S(1)} %sum.1.refs_0_, f32[8,128]{1,0:T(8,128)S(1)} %collective-permute-done.23.refs_1_, f32[8,128]{1,0:T(8,128)S(1)} %collective-permute-done.24.refs_2_, ...), custom_call_target="tpu_custom_call" | custom-call | tf_op jit(solution)/shard_map/last/pallas_call | solution.py:465
  (18 shorter events, 1.0 us)
Async XLA Ops:
  2.8 17.3 %collective-permute-start.4 = (f32[616,128]{1,0:T(8,128)S(1)}, f32[616,128]{1,0:T(8,128)S(1)}, u32[]{:S(2)}, u32[]{:S(2)}) collective-permute-start(f32[616,128]{1,0:T(8,128)S(1)} %get-tuple-element.36.refs_2_), channel_id=1, source_target_pairs={{0,1},{1,0},{2,3},{3,2},{4,5},{5,4},{6,7},{7,6},{8,9},{9,8},{10,11... | collective-permute-start | bytes 946184 | tf_op jit(solution)/shard_map/ppermute | solution.py:479
  3.4 6.8 %collective-permute-start.2 = (f32[72,128]{1,0:T(8,128)S(1)}, f32[72,128]{1,0:T(8,128)S(1)}, u32[]{:S(2)}, u32[]{:S(2)}) collective-permute-start(f32[72,128]{1,0:T(8,128)S(1)} %get-tuple-element.35.refs_0_), channel_id=1, source_target_pairs={{0,6},{1,7},{2,4},{3,5},{4,2},{5,3},{6,0},{7,1},{8,14},{9,15},{10,... | collective-permute-start | bytes 110600 | tf_op jit(solution)/shard_map/ppermute | solution.py:479
  8.0 4.9 %collective-permute-start.1 = (f32[72,128]{1,0:T(8,128)S(1)}, f32[72,128]{1,0:T(8,128)S(1)}, u32[]{:S(2)}, u32[]{:S(2)}) collective-permute-start(f32[72,128]{1,0:T(8,128)S(1)} %get-tuple-element.35.refs_0_), channel_id=1, source_target_pairs={{0,4},{1,5},{2,6},{3,7},{4,0},{5,1},{6,2},{7,3},{8,12},{9,13},{10,... | collective-permute-start | bytes 110600 | tf_op jit(solution)/shard_map/ppermute | solution.py:479
  8.0 4.9 %collective-permute-start = (f32[72,128]{1,0:T(8,128)S(1)}, f32[72,128]{1,0:T(8,128)S(1)}, u32[]{:S(2)}, u32[]{:S(2)}) collective-permute-start(f32[72,128]{1,0:T(8,128)S(1)} %get-tuple-element.35.refs_0_), channel_id=1, source_target_pairs={{0,2},{1,3},{2,0},{3,1},{4,6},{5,7},{6,4},{7,5},{8,10},{9,11},{10,... | collective-permute-start | bytes 110600 | tf_op jit(solution)/shard_map/ppermute | solution.py:479
  12.9 1.4 %collective-permute-start.3 = (f32[272,128]{1,0:T(8,128)S(1)}, f32[272,128]{1,0:T(8,128)S(1)}, u32[]{:S(2)}, u32[]{:S(2)}) collective-permute-start(f32[272,128]{1,0:T(8,128)S(1)} %chip.1.refs_0_.own_ref), channel_id=1, source_target_pairs={{0,1},{1,0},{2,3},{3,2},{4,5},{5,4},{6,7},{7,6},{8,9},{9,8},{10,11... | collective-permute-start | bytes 417800 | tf_op jit(solution)/shard_map/ppermute | solution.py:479
  14.4 6.3 %collective-permute-start.7 = (f32[16,128]{1,0:T(8,128)S(1)}, f32[16,128]{1,0:T(8,128)S(1)}, u32[]{:S(2)}, u32[]{:S(2)}) collective-permute-start(f32[16,128]{1,0:T(8,128)S(1)} %group.3.refs_11_), channel_id=1, source_target_pairs={{0,24},{8,16},{16,8},{24,0},{1,25},{9,17},{17,9},{25,1},{2,26},{10... | collective-permute-start | bytes 24584 | tf_op jit(solution)/shard_map/ppermute | solution.py:479
  16.9 3.8 %collective-permute-start.6 = (f32[16,128]{1,0:T(8,128)S(1)}, f32[16,128]{1,0:T(8,128)S(1)}, u32[]{:S(2)}, u32[]{:S(2)}) collective-permute-start(f32[16,128]{1,0:T(8,128)S(1)} %group.3.refs_11_), channel_id=1, source_target_pairs={{0,16},{8,24},{16,0},{24,8},{1,17},{9,25},{17,1},{25,9},{2,18},{10... | collective-permute-start | bytes 24584 | tf_op jit(solution)/shard_map/ppermute | solution.py:479
  17.4 3.7 %collective-permute-start.5 = (f32[16,128]{1,0:T(8,128)S(1)}, f32[16,128]{1,0:T(8,128)S(1)}, u32[]{:S(2)}, u32[]{:S(2)}) collective-permute-start(f32[16,128]{1,0:T(8,128)S(1)} %group.3.refs_11_), channel_id=1, source_target_pairs={{0,8},{8,0},{16,24},{24,16},{1,9},{9,1},{17,25},{25,17},{2,10},{10... | collective-permute-start | bytes 24584 | tf_op jit(solution)/shard_map/ppermute | solution.py:479
  22.7 5.6 %collective-permute-start.10 = (f32[32,128]{1,0:T(8,128)S(1)}, f32[32,128]{1,0:T(8,128)S(1)}, u32[]{:S(2)}, u32[]{:S(2)}) collective-permute-start(f32[32,128]{1,0:T(8,128)S(1)} %get-tuple-element.45.refs_0_), channel_id=1, source_target_pairs={{0,6},{1,7},{2,4},{3,5},{4,2},{5,3},{6,0},{7,1},{8,14},{9,15},{10,... | collective-permute-start | bytes 49160 | tf_op jit(solution)/shard_map/ppermute | solution.py:479
  24.5 4.6 %collective-permute-start.9 = (f32[32,128]{1,0:T(8,128)S(1)}, f32[32,128]{1,0:T(8,128)S(1)}, u32[]{:S(2)}, u32[]{:S(2)}) collective-permute-start(f32[32,128]{1,0:T(8,128)S(1)} %get-tuple-element.45.refs_0_), channel_id=1, source_target_pairs={{0,4},{1,5},{2,6},{3,7},{4,0},{5,1},{6,2},{7,3},{8,12},{9,13},{10,... | collective-permute-start | bytes 49160 | tf_op jit(solution)/shard_map/ppermute | solution.py:479
  24.8 4.3 %collective-permute-start.8 = (f32[32,128]{1,0:T(8,128)S(1)}, f32[32,128]{1,0:T(8,128)S(1)}, u32[]{:S(2)}, u32[]{:S(2)}) collective-permute-start(f32[32,128]{1,0:T(8,128)S(1)} %get-tuple-element.45.refs_0_), channel_id=1, source_target_pairs={{0,2},{1,3},{2,0},{3,1},{4,6},{5,7},{6,4},{7,5},{8,10},{9,11},{10,... | collective-permute-start | bytes 49160 | tf_op jit(solution)/shard_map/ppermute | solution.py:479
  29.2 5.1 %collective-permute-start.13 = (f32[16,128]{1,0:T(8,128)S(1)}, f32[16,128]{1,0:T(8,128)S(1)}, u32[]{:S(2)}, u32[]{:S(2)}) collective-permute-start(f32[16,128]{1,0:T(8,128)S(1)} %get-tuple-element.52.refs_16_), channel_id=1, source_target_pairs={{0,24},{8,16},{16,8},{24,0},{1,25},{9,17},{17,9},{25,1},{2,26},{10... | collective-permute-start | bytes 24584 | tf_op jit(solution)/shard_map/ppermute | solution.py:479
  31.4 3.7 %collective-permute-start.12 = (f32[16,128]{1,0:T(8,128)S(1)}, f32[16,128]{1,0:T(8,128)S(1)}, u32[]{:S(2)}, u32[]{:S(2)}) collective-permute-start(f32[16,128]{1,0:T(8,128)S(1)} %get-tuple-element.52.refs_16_), channel_id=1, source_target_pairs={{0,16},{8,24},{16,0},{24,8},{1,17},{9,25},{17,1},{25,9},{2,18},{10... | collective-permute-start | bytes 24584 | tf_op jit(solution)/shard_map/ppermute | solution.py:479
  31.9 3.7 %collective-permute-start.11 = (f32[16,128]{1,0:T(8,128)S(1)}, f32[16,128]{1,0:T(8,128)S(1)}, u32[]{:S(2)}, u32[]{:S(2)}) collective-permute-start(f32[16,128]{1,0:T(8,128)S(1)} %get-tuple-element.52.refs_16_), channel_id=1, source_target_pairs={{0,8},{8,0},{16,24},{24,16},{1,9},{9,1},{17,25},{25,17},{2,10},{10... | collective-permute-start | bytes 24584 | tf_op jit(solution)/shard_map/ppermute | solution.py:479
  37.2 5.6 %collective-permute-start.16 = (f32[32,128]{1,0:T(8,128)S(1)}, f32[32,128]{1,0:T(8,128)S(1)}, u32[]{:S(2)}, u32[]{:S(2)}) collective-permute-start(f32[32,128]{1,0:T(8,128)S(1)} %get-tuple-element.53.refs_0_), channel_id=1, source_target_pairs={{0,6},{1,7},{2,4},{3,5},{4,2},{5,3},{6,0},{7,1},{8,14},{9,15},{10,... | collective-permute-start | bytes 49160 | tf_op jit(solution)/shard_map/ppermute | solution.py:479
  39.5 4.7 %collective-permute-start.15 = (f32[32,128]{1,0:T(8,128)S(1)}, f32[32,128]{1,0:T(8,128)S(1)}, u32[]{:S(2)}, u32[]{:S(2)}) collective-permute-start(f32[32,128]{1,0:T(8,128)S(1)} %get-tuple-element.53.refs_0_), channel_id=1, source_target_pairs={{0,4},{1,5},{2,6},{3,7},{4,0},{5,1},{6,2},{7,3},{8,12},{9,13},{10,... | collective-permute-start | bytes 49160 | tf_op jit(solution)/shard_map/ppermute | solution.py:479
  40.4 3.9 %collective-permute-start.14 = (f32[32,128]{1,0:T(8,128)S(1)}, f32[32,128]{1,0:T(8,128)S(1)}, u32[]{:S(2)}, u32[]{:S(2)}) collective-permute-start(f32[32,128]{1,0:T(8,128)S(1)} %get-tuple-element.53.refs_0_), channel_id=1, source_target_pairs={{0,2},{1,3},{2,0},{3,1},{4,6},{5,7},{6,4},{7,5},{8,10},{9,11},{10,... | collective-permute-start | bytes 49160 | tf_op jit(solution)/shard_map/ppermute | solution.py:479
  44.3 5.1 %collective-permute-start.19 = (f32[16,128]{1,0:T(8,128)S(1)}, f32[16,128]{1,0:T(8,128)S(1)}, u32[]{:S(2)}, u32[]{:S(2)}) collective-permute-start(f32[16,128]{1,0:T(8,128)S(1)} %get-tuple-element.60.refs_16_), channel_id=1, source_target_pairs={{0,24},{8,16},{16,8},{24,0},{1,25},{9,17},{17,9},{25,1},{2,26},{10... | collective-permute-start | bytes 24584 | tf_op jit(solution)/shard_map/ppermute | solution.py:479
  46.2 3.7 %collective-permute-start.18 = (f32[16,128]{1,0:T(8,128)S(1)}, f32[16,128]{1,0:T(8,128)S(1)}, u32[]{:S(2)}, u32[]{:S(2)}) collective-permute-start(f32[16,128]{1,0:T(8,128)S(1)} %get-tuple-element.60.refs_16_), channel_id=1, source_target_pairs={{0,16},{8,24},{16,0},{24,8},{1,17},{9,25},{17,1},{25,9},{2,18},{10... | collective-permute-start | bytes 24584 | tf_op jit(solution)/shard_map/ppermute | solution.py:479
  46.7 3.7 %collective-permute-start.17 = (f32[16,128]{1,0:T(8,128)S(1)}, f32[16,128]{1,0:T(8,128)S(1)}, u32[]{:S(2)}, u32[]{:S(2)}) collective-permute-start(f32[16,128]{1,0:T(8,128)S(1)} %get-tuple-element.60.refs_16_), channel_id=1, source_target_pairs={{0,8},{8,0},{16,24},{24,16},{1,9},{9,1},{17,25},{25,17},{2,10},{10... | collective-permute-start | bytes 24584 | tf_op jit(solution)/shard_map/ppermute | solution.py:479
  51.5 5.4 %collective-permute-start.22 = (f32[8,128]{1,0:T(8,128)S(1)}, f32[8,128]{1,0:T(8,128)S(1)}, u32[]{:S(2)}, u32[]{:S(2)}) collective-permute-start(f32[8,128]{1,0:T(8,128)S(1)} %get-tuple-element.62.refs_0_), channel_id=1, source_target_pairs={{0,6},{1,7},{2,4},{3,5},{4,2},{5,3},{6,0},{7,1},{8,14},{9,15},{10,... | collective-permute-start | bytes 12296 | tf_op jit(solution)/shard_map/ppermute | solution.py:479
  53.1 4.5 %collective-permute-start.21 = (f32[8,128]{1,0:T(8,128)S(1)}, f32[8,128]{1,0:T(8,128)S(1)}, u32[]{:S(2)}, u32[]{:S(2)}) collective-permute-start(f32[8,128]{1,0:T(8,128)S(1)} %get-tuple-element.62.refs_0_), channel_id=1, source_target_pairs={{0,4},{1,5},{2,6},{3,7},{4,0},{5,1},{6,2},{7,3},{8,12},{9,13},{10,... | collective-permute-start | bytes 12296 | tf_op jit(solution)/shard_map/ppermute | solution.py:479
  54.0 3.6 %collective-permute-start.20 = (f32[8,128]{1,0:T(8,128)S(1)}, f32[8,128]{1,0:T(8,128)S(1)}, u32[]{:S(2)}, u32[]{:S(2)}) collective-permute-start(f32[8,128]{1,0:T(8,128)S(1)} %get-tuple-element.62.refs_0_), channel_id=1, source_target_pairs={{0,2},{1,3},{2,0},{3,1},{4,6},{5,7},{6,4},{7,5},{8,10},{9,11},{10,... | collective-permute-start | bytes 12296 | tf_op jit(solution)/shard_map/ppermute | solution.py:479
  57.7 4.5 %collective-permute-start.25 = (f32[8,128]{1,0:T(8,128)S(1)}, f32[8,128]{1,0:T(8,128)S(1)}, u32[]{:S(2)}, u32[]{:S(2)}) collective-permute-start(f32[8,128]{1,0:T(8,128)S(1)} %sum.1.refs_0_), channel_id=1, source_target_pairs={{0,24},{8,16},{16,8},{24,0},{1,25},{9,17},{17,9},{25,1},{2,26},{10... | collective-permute-start | bytes 12296 | tf_op jit(solution)/shard_map/ppermute | solution.py:479
  59.8 3.6 %collective-permute-start.24 = (f32[8,128]{1,0:T(8,128)S(1)}, f32[8,128]{1,0:T(8,128)S(1)}, u32[]{:S(2)}, u32[]{:S(2)}) collective-permute-start(f32[8,128]{1,0:T(8,128)S(1)} %sum.1.refs_0_), channel_id=1, source_target_pairs={{0,16},{8,24},{16,0},{24,8},{1,17},{9,25},{17,1},{25,9},{2,18},{10... | collective-permute-start | bytes 12296 | tf_op jit(solution)/shard_map/ppermute | solution.py:479
  60.3 3.6 %collective-permute-start.23 = (f32[8,128]{1,0:T(8,128)S(1)}, f32[8,128]{1,0:T(8,128)S(1)}, u32[]{:S(2)}, u32[]{:S(2)}) collective-permute-start(f32[8,128]{1,0:T(8,128)S(1)} %sum.1.refs_0_), channel_id=1, source_target_pairs={{0,8},{8,0},{16,24},{24,16},{1,9},{9,1},{17,25},{25,17},{2,10},{10... | collective-permute-start | bytes 12296 | tf_op jit(solution)/shard_map/ppermute | solution.py:479
